TPU v7x, 512 devices: a whole 4x4x16 slice. The times are simulated.
512 devices in a mesh: sec: 16 (over z), slab: 32 (over y, x, core).
Axes of the slice: x: 4, y: 4, z: 16, core: 2. Of those that a mesh axis runs over, the one named last changes fastest.
Arguments:
- heat_level: float32 [16, 128, 64, 128], P('sec', 'slab'), may hold values from -6 to 6
- material_factor: float32 [16, 128, 64, 128], P('sec', 'slab'), may hold values from 0.4 to 1.2
- dual_sensitivity: float32 [16, 128, 64, 128], P('sec', 'slab'), may hold values from -6 to 6
- source_liquid_part: int32 [4, 48, 1], replicated, may hold values from 0 to 11; in each aligned block of 48 rows (0 to 47, 48 to 95, ..., all dimensions but the last counted through in order) at most 8 rows name the same one
- source_liquid_line: int32 [4, 48], replicated, may hold values from 0 to 63
- solid_touch_flag: int32 [4, 48], replicated, may hold values 0 or 1
- archived_instant: int32 [1], replicated, may hold values from 0 to 63
Outputs:
- state_field: float32 [16, 128, 64, 128], P('sec', 'slab')
- adjoint_field: float32 [16, 128, 64, 128], P('sec', 'slab')
Inputs may be any that keep to these rules, and one draw needn't show every extreme that they name: `source_liquid_part`: among the 48 rows of one ingot section no melt section is named more than 8 times, and in some ingot section one melt section is named exactly 8 times.
All inputs are finite; a program needn't handle non-finite values.
Results may differ from a plain program's by a relative error of at most 0.0002.
Values sent between devices are 32-bit elements; how exact they have to be, the bound alone decides.
A program may use at most 64 MiB of HBM per device.

v0:
```python
import math

import jax
import jax.numpy as jnp
from jax import lax
from jax.sharding import PartitionSpec as P

STEPS = 4
ITERS = 4
PAIRCAP = 8


time_step = 0.1
sink_rate = 0.5
period_steps = 16.0


def extended(array, sides, width):
    for axis, dim in sides:
        count, length = (lax.axis_size(axis), array.shape[dim])
        up = [(i, (i + 1) % count) for i in range(count - 1)]
        down = [(j, i) for i, j in up]
        last = lax.slice_in_dim(array, length - width, length, axis=dim)
        first = lax.slice_in_dim(array, 0, width, axis=dim)
        before = lax.ppermute(last, axis, up)
        after = lax.ppermute(first, axis, down)
        array = jnp.concatenate([before, array, after], axis=dim)
    return array


def neighbor_sum(padded):
    center = padded[..., 1:-1, :, :]
    widths = [(0, 0)] * (center.ndim - 2) + [(1, 1), (1, 1)]
    plane_cycle = jnp.pad(center, widths)
    total = padded[..., 2:, :, :] + padded[..., :-2, :, :]
    total = total + plane_cycle[..., 2:, 1:-1] + plane_cycle[..., :-2, 1:-1]
    return total + plane_cycle[..., 1:-1, 2:] + plane_cycle[..., 1:-1, :-2]


def pull_speed(archived_instant, substep):
    phase = archived_instant[0].astype(jnp.float32) + substep
    return 1.0 + 0.5 * jnp.sin(2.0 * math.pi * phase / period_steps)


def melt_advance(padded, factor, velocity):
    center = padded[..., 1:-1, :, :]
    neighbors = neighbor_sum(padded)
    change = factor * (neighbors - 6.0 * center) - velocity * (center - padded[..., :-2, :, :])
    return center + time_step * change - time_step * sink_rate * jnp.tanh(center)


def melt_reverse(weighted_pad, adjoint_pad, melt_adjoint, earlier, velocity):
    weighted = weighted_pad[..., 1:-1, :, :]
    neighbors = neighbor_sum(weighted_pad)
    change = neighbors - 6.0 * weighted - velocity * (melt_adjoint - adjoint_pad[..., 2:, :, :])
    slope = 1.0 - jnp.tanh(earlier) ** 2
    return melt_adjoint + time_step * change - time_step * sink_rate * slope * melt_adjoint


def apply_operator(vector, factor):
    padded = extended(vector, (("slab", 0),), 1)
    center = padded[1:-1]
    return (6.0 + factor) * center - neighbor_sum(padded)


def squares(residual):
    return lax.psum(jnp.sum(residual * residual), "slab")


def conjugate(right_side, factor):
    solution = jnp.zeros_like(right_side)
    residual = right_side
    direction = right_side
    norm_now = squares(residual)
    for iteration in range(ITERS):
        applied = apply_operator(direction, factor)
        curvature = lax.psum(jnp.sum(direction * applied), "slab")
        step_size = norm_now / curvature
        solution = solution + step_size * direction
        residual = residual - step_size * applied
        norm_next = squares(residual)
        direction = residual + norm_next / norm_now * direction
        norm_now = norm_next
    return solution


def body(
    heat_level,
    material_factor,
    dual_sensitivity,
    source_liquid_part,
    source_liquid_line,
    solid_touch_flag,
    archived_instant,
):
    nearby_heat_level = heat_level[0]
    own_coefficient = material_factor[0]
    own_cotangent = dual_sensitivity[0]
    layer_pile, horizontal_sum, vertical_sum = nearby_heat_level.shape
    sec_count = lax.axis_size("sec")
    sections = source_liquid_part[:, :, 0]
    ingot_count, contact_rows = sections.shape
    melt_count = sec_count - ingot_count
    my_section = lax.axis_index("sec")
    is_melt = my_section < melt_count
    own_ingot = jnp.clip(my_section - melt_count, 0, ingot_count - 1)
    states = []
    current_entry = nearby_heat_level
    for substep in range(STEPS):
        states.append(current_entry)
        padded = extended(current_entry, (("slab", 0),), 1)
        current_entry = melt_advance(padded, own_coefficient, pull_speed(archived_instant, substep))
    ordinal = jnp.arange(contact_rows)
    same_source = (sections[:, :, None] == sections[:, None, :]) & (
        ordinal[None, None, :] < ordinal[None, :, None]
    )
    slot_rank = jnp.sum(same_source.astype(jnp.int32), axis=2)
    slot_ids = jnp.arange(PAIRCAP)
    chosen = (sections[:, None, :] == my_section) & (
        slot_rank[:, None, :] == slot_ids[None, :, None]
    )
    slot_row = jnp.sum(jnp.where(chosen, source_liquid_line[:, None, :], 0), axis=2)
    slot_live = jnp.any(chosen, axis=2).astype(jnp.float32)
    offered = (
        jnp.take(current_entry, slot_row.reshape(-1), axis=1) * slot_live.reshape(-1)[None, :, None]
    )
    own_sections = lax.dynamic_index_in_dim(sections, own_ingot, 0, keepdims=False)
    own_rank = lax.dynamic_index_in_dim(slot_rank, own_ingot, 0, keepdims=False)
    own_contact = lax.dynamic_index_in_dim(solid_touch_flag, own_ingot, 0, keepdims=False).astype(
        jnp.float32
    )
    gathered = lax.all_gather(offered[None], "sec", axis=0, tiled=True)
    solid_interface = gathered[own_sections, :, own_ingot * PAIRCAP + own_rank, :]
    placed = own_contact[None, :, None] * jnp.transpose(solid_interface, (1, 0, 2))
    heat_strain_source = nearby_heat_level + jnp.pad(
        placed, ((0, 0), (0, horizontal_sum - contact_rows), (0, 0))
    )
    displacement = conjugate(heat_strain_source, own_coefficient)
    adjoint_ingot = conjugate(own_cotangent, own_coefficient)
    sensitivity = jnp.where(
        is_melt, 0.0, own_contact[None, :, None] * adjoint_ingot[:, :contact_rows, :]
    )
    row_onehot = (
        source_liquid_line[:, :, None] == jnp.arange(horizontal_sum)[None, None, :]
    ).astype(jnp.float32)
    returned_rows = lax.all_gather(sensitivity[None], "sec", axis=0, tiled=True)
    targets = (sections == my_section).astype(jnp.float32)[:, :, None] * row_onehot
    returned_sum = jnp.einsum(
        "jzrc,jrq->zqc", returned_rows[melt_count:], targets, precision=lax.Precision.HIGHEST
    )
    melt_adjoint = own_cotangent + returned_sum
    for substep in reversed(range(STEPS)):
        stacked = jnp.stack([own_coefficient * melt_adjoint, melt_adjoint])
        widened = extended(stacked, (("slab", 1),), 1)
        melt_adjoint = melt_reverse(
            widened[0],
            widened[1],
            melt_adjoint,
            states[substep],
            pull_speed(archived_instant, substep),
        )
    state_field = jnp.where(is_melt, current_entry, displacement)[None]
    adjoint_field = jnp.where(is_melt, melt_adjoint, adjoint_ingot)[None]
    return (state_field, adjoint_field)


def solution(mesh):
    in_specs = (
        P("sec", "slab", None, None),
        P("sec", "slab", None, None),
        P("sec", "slab", None, None),
        P(),
        P(),
        P(),
        P(),
    )
    out_specs = (P("sec", "slab", None, None), P("sec", "slab", None, None))
    return jax.shard_map(body, mesh=mesh, in_specs=in_specs, out_specs=out_specs, check_vma=False)
```

profile of v0, /device:TPU:1, one launch (start us, length us, event | category | flops | bytes accessed | tf_op | source)
XLA Modules:
  0.0 760.2 jit_solution(5622631248806299823)
XLA Ops:
  7.2 0.8 slice_bitcast_fusion.1
  8.0 4.5 collective-permute-start.17
  12.5 5.6 collective-permute-start.16
  18.1 0.8 slice_bitcast_fusion.3
  18.9 1.9 collective-permute-start.1
  20.8 2.4 collective-permute-start
  23.2 1.0 convert_reduce_fusion
  24.9 0.8 select_reduce_fusion
  26.7 1.8 fusion.10
  28.5 3.2 collective-permute-start.3
  31.7 1.9 collective-permute-start.2
  33.7 3.2 collective-permute-done.2
  36.9 2.6 multiply_reduce_fusion.5
  39.5 1.9 collective-permute-start.5
  41.4 2.4 collective-permute-start.4
  44.1 2.6 collective-permute-done.4
  46.8 1.9 collective-permute-start.7
  48.7 2.4 collective-permute-start.6
  51.3 2.6 collective-permute-done.6
  56.3 73.0 %all-gather.4.cloned.1.call-done = f32[16,4,32,128]{3,2,1,0:T(8,128)} async-done(((f32[1,4,32,128]{3,2,1,0:T(8,128)}), f32[16,4,32,128]{3,2,1,0:T(8,128)}) %all-gather.4.cloned.1.call-update) | async-done | bytes 1048592 | tf_op jit(solution)/shard_map/all_gather | solution.py:132
  129.3 1.9 copy.24
  131.2 0.9 gather_fusion.1
  132.3 13.1 %collective-permute-start.9 = (f32[1,64,128]{2,1,0:T(8,128)S(1)}, f32[1,64,128]{2,1,0:T(8,128)S(1)}, u32[]{:S(2)}, u32[]{:S(2)}) collective-permute-start(f32[1,64,128]{2,1,0:T(8,128)S(1)} %get-tuple-element.72), channel_id=1, source_target_pairs={{0,1},{1,2},{2,3},{3,4},{4,5},{5,6},{6,7},{7,8},{8,9},{9,10},{10,1... | collective-permute-start | bytes 98312 | tf_op jit(solution)/shard_map/ppermute | solution.py:25
  145.4 1.9 collective-permute-start.8
  147.3 3.3 collective-permute-done.8
  150.6 0.8 multiply_reduce_fusion.12
  151.4 61.6 %all-reduce.23 = (f32[]{:T(128)}, f32[]{:T(128)}, f32[]{:T(128)}, f32[]{:T(128)}) all-reduce(f32[]{:T(128)} %get-tuple-element.7, f32[]{:T(128)} %get-tuple-element.6, f32[]{:T(128)} %get-tuple-element.5, f32[]{:T(128)} %get-tuple-element.4), channel_id=1, replica_groups=mesh['sec'=16,'slab'=32] {'slab'}, use_global_device_ids=true, to_apply=%region_4.5 | all-reduce | flops 4 | bytes 32 | tf_op jit(solution)/shard_map/psum | solution.py:67
  216.3 65.9 %all-reduce.22 = (f32[]{:T(128)}, f32[]{:T(128)}) all-reduce(f32[]{:T(128)} %get-tuple-element.84, f32[]{:T(128)} %get-tuple-element.83), channel_id=1, replica_groups=mesh['sec'=16,'slab'=32] {'slab'}, use_global_device_ids=true, to_apply=%region_8.9 | all-reduce | flops 2 | bytes 16 | tf_op jit(solution)/shard_map/psum | solution.py:67
  283.5 1.9 collective-permute-start.19
  285.4 2.4 collective-permute-start.18
  289.1 3.2 collective-permute-start.11
  292.2 1.9 collective-permute-start.10
  294.2 3.3 collective-permute-done.10
  297.5 0.9 multiply_reduce_fusion.3
  298.4 60.4 %all-reduce.21 = (f32[]{:T(128)}, f32[]{:T(128)}) all-reduce(f32[]{:T(128)} %get-tuple-element.62, f32[]{:T(128)} %get-tuple-element.38), channel_id=1, replica_groups=mesh['sec'=16,'slab'=32] {'slab'}, use_global_device_ids=true, to_apply=%region_10.11 | all-reduce | flops 2 | bytes 16 | tf_op jit(solution)/shard_map/psum | solution.py:77
  362.6 65.8 %all-reduce.20 = (f32[]{:T(128)}, f32[]{:T(128)}) all-reduce(f32[]{:T(128)} %get-tuple-element.36, f32[]{:T(128)} %get-tuple-element.34), channel_id=1, replica_groups=mesh['sec'=16,'slab'=32] {'slab'}, use_global_device_ids=true, to_apply=%region_12.13 | all-reduce | flops 2 | bytes 16 | tf_op jit(solution)/shard_map/psum | solution.py:67
  431.1 1.9 collective-permute-start.21
  433.0 2.4 collective-permute-start.20
  435.4 3.2 collective-permute-start.13
  438.6 1.9 collective-permute-start.12
  440.6 3.3 collective-permute-done.12
  443.8 0.8 multiply_reduce_fusion.1
  444.7 60.6 %all-reduce.19 = (f32[]{:T(128)}, f32[]{:T(128)}) all-reduce(f32[]{:T(128)} %get-tuple-element.56, f32[]{:T(128)} %get-tuple-element.30), channel_id=1, replica_groups=mesh['sec'=16,'slab'=32] {'slab'}, use_global_device_ids=true, to_apply=%region_14.15 | all-reduce | flops 2 | bytes 16 | tf_op jit(solution)/shard_map/psum | solution.py:77
  509.1 65.9 %all-reduce.18 = (f32[]{:T(128)}, f32[]{:T(128)}) all-reduce(f32[]{:T(128)} %multiply_reduce_fusion.7, f32[]{:T(128)} %multiply_reduce_fusion), channel_id=1, replica_groups=mesh['sec'=16,'slab'=32] {'slab'}, use_global_device_ids=true, to_apply=%region_16.17 | all-reduce | flops 2 | bytes 16 | tf_op jit(solution)/shard_map/psum | solution.py:67
  576.4 1.9 collective-permute-start.23
  578.3 2.4 collective-permute-start.22
  582.0 3.2 collective-permute-start.15
  585.2 1.9 collective-permute-start.14
  587.1 3.3 collective-permute-done.14
  590.4 0.8 fusion.161
  591.2 60.6 %all-reduce.17 = (f32[]{:T(128)}, f32[]{:T(128)}) all-reduce(f32[]{:T(128)} %get-tuple-element.3, f32[]{:T(128)} %get-tuple-element.2), channel_id=1, replica_groups=mesh['sec'=16,'slab'=32] {'slab'}, use_global_device_ids=true, to_apply=%region_18.19 | all-reduce | flops 2 | bytes 16 | tf_op jit(solution)/shard_map/psum | solution.py:77
  653.9 57.5 %all-gather.6.cloned.1.call-done = f32[64,48,128]{2,1,0:T(8,128)} async-done(((f32[4,48,128]{2,1,0:T(8,128)}), f32[64,48,128]{2,1,0:T(8,128)}) %all-gather.6.cloned.1.call-update) | async-done | bytes 1572880 | tf_op jit(solution)/shard_map/all_gather | solution.py:146
  711.4 1.0 slice.682
  713.0 12.2 %collective-permute-start.24 = (f32[2,1,64,128]{3,2,1,0:T(8,128)S(1)}, f32[2,1,64,128]{3,2,1,0:T(8,128)S(1)}, u32[]{:S(2)}, u32[]{:S(2)}) collective-permute-start(f32[2,1,64,128]{3,2,1,0:T(8,128)S(1)} %get-tuple-element.51), channel_id=1, source_target_pairs={{1,0},{2,1},{3,2},{4,3},{5,4},{6,5},{7,6},{8,7},{9,8},{10,9},{11,1... | collective-permute-start | bytes 196616 | tf_op jit(solution)/shard_map/ppermute | solution.py:26
  725.2 3.0 collective-permute-start.25
  728.2 1.3 collective-permute-done.25
  729.7 1.9 collective-permute-start.26
  731.6 4.3 collective-permute-start.27
  735.9 1.3 collective-permute-done.27
  737.4 1.9 collective-permute-start.28
  739.3 4.3 collective-permute-start.29
  745.1 1.9 collective-permute-start.30
  747.0 4.3 collective-permute-start.31
  752.6 0.8 fusion.120
  (89 shorter events, 10.5 us)
Async XLA Ops:
  7.2 39.5 %copy-start = (f32[1,4,64,128]{3,2,1,0:T(8,128)S(1)}, f32[1,4,64,128]{3,2,1,0:T(8,128)}, u32[]{:S(2)}) copy-start(f32[1,4,64,128]{3,2,1,0:T(8,128)} %param.8) | copy-start | bytes 393220
  7.2 122.1 %all-gather.4.cloned.1.call-start = ((), (), s32[]{:S(2)}) async-start(), calls=%async_computation | async-start | bytes 1114112 | tf_op jit(solution)/shard_map/all_gather | solution.py:132
  8.0 25.7 %collective-permute-start.17 = (f32[1,64,128]{2,1,0:T(8,128)S(1)}, f32[1,64,128]{2,1,0:T(8,128)S(1)}, u32[]{:S(2)}, u32[]{:S(2)}) collective-permute-start(f32[1,64,128]{2,1,0:T(8,128)S(1)} %get-tuple-element.70), channel_id=1, source_target_pairs={{0,1},{1,2},{2,3},{3,4},{4,5},{5,6},{6,7},{7,8},{8,9},{9,10},{10,1... | collective-permute-start | bytes 98312 | tf_op jit(solution)/shard_map/ppermute | solution.py:25
  12.5 21.2 %collective-permute-start.16 = (f32[1,64,128]{2,1,0:T(8,128)S(1)}, f32[1,64,128]{2,1,0:T(8,128)S(1)}, u32[]{:S(2)}, u32[]{:S(2)}) collective-permute-start(f32[1,64,128]{2,1,0:T(8,128)S(1)} %get-tuple-element.69), channel_id=1, source_target_pairs={{1,0},{2,1},{3,2},{4,3},{5,4},{6,5},{7,6},{8,7},{9,8},{10,9},{11,1... | collective-permute-start | bytes 98312 | tf_op jit(solution)/shard_map/ppermute | solution.py:26
  18.9 7.8 %collective-permute-start.1 = (f32[1,64,128]{2,1,0:T(8,128)S(1)}, f32[1,64,128]{2,1,0:T(8,128)S(1)}, u32[]{:S(2)}, u32[]{:S(2)}) collective-permute-start(f32[1,64,128]{2,1,0:T(8,128)S(1)} %get-tuple-element.80), channel_id=1, source_target_pairs={{0,1},{1,2},{2,3},{3,4},{4,5},{5,6},{6,7},{7,8},{8,9},{9,10},{10,1... | collective-permute-start | bytes 98312 | tf_op jit(solution)/shard_map/ppermute | solution.py:25
  20.8 5.9 collective-permute-start
  26.7 28.9 %copy-start.3 = (s32[4,48,1]{1,2,0:T(1,128)S(1)}, s32[4,48,1]{1,2,0:T(1,128)}, u32[]{:S(2)}) copy-start(s32[4,48,1]{1,2,0:T(1,128)} %param.10) | copy-start | bytes 2308
  28.5 5.2 collective-permute-start.3
  31.7 5.2 collective-permute-start.2
  39.5 4.6 collective-permute-start.5
  41.4 5.2 collective-permute-start.4
  46.8 4.5 collective-permute-start.7
  48.7 5.2 collective-permute-start.6
  54.1 78.1 %copy-start.2 = (f32[1,4,64,128]{3,2,1,0:T(8,128)S(1)}, f32[1,4,64,128]{3,2,1,0:T(8,128)}, u32[]{:S(2)}) copy-start(f32[1,4,64,128]{3,2,1,0:T(8,128)} %param.7) | copy-start | bytes 393220
  55.6 655.9 %all-gather.6.cloned.1.call-start = ((), (), s32[]{:S(2)}) async-start(), calls=%async_computation.1 | async-start | bytes 1671168 | tf_op jit(solution)/shard_map/all_gather | solution.py:146
  56.3 159.2 %copy-start.1 = (f32[1,4,64,128]{3,2,1,0:T(8,128)S(1)}, f32[1,4,64,128]{3,2,1,0:T(8,128)}, u32[]{:S(2)}) copy-start(f32[1,4,64,128]{3,2,1,0:T(8,128)} %param.9) | copy-start | bytes 393220
  132.3 15.0 %collective-permute-start.9 = (f32[1,64,128]{2,1,0:T(8,128)S(1)}, f32[1,64,128]{2,1,0:T(8,128)S(1)}, u32[]{:S(2)}, u32[]{:S(2)}) collective-permute-start(f32[1,64,128]{2,1,0:T(8,128)S(1)} %get-tuple-element.72), channel_id=1, source_target_pairs={{0,1},{1,2},{2,3},{3,4},{4,5},{5,6},{6,7},{7,8},{8,9},{9,10},{10,1... | collective-permute-start | bytes 98312 | tf_op jit(solution)/shard_map/ppermute | solution.py:25
  145.4 5.2 collective-permute-start.8
  283.5 10.7 %collective-permute-start.19 = (f32[1,64,128]{2,1,0:T(8,128)S(1)}, f32[1,64,128]{2,1,0:T(8,128)S(1)}, u32[]{:S(2)}, u32[]{:S(2)}) collective-permute-start(f32[1,64,128]{2,1,0:T(8,128)S(1)} %get-tuple-element.65), channel_id=1, source_target_pairs={{0,1},{1,2},{2,3},{3,4},{4,5},{5,6},{6,7},{7,8},{8,9},{9,10},{10,1... | collective-permute-start | bytes 98312 | tf_op jit(solution)/shard_map/ppermute | solution.py:25
  285.4 8.8 %collective-permute-start.18 = (f32[1,64,128]{2,1,0:T(8,128)S(1)}, f32[1,64,128]{2,1,0:T(8,128)S(1)}, u32[]{:S(2)}, u32[]{:S(2)}) collective-permute-start(f32[1,64,128]{2,1,0:T(8,128)S(1)} %get-tuple-element.64), channel_id=1, source_target_pairs={{1,0},{2,1},{3,2},{4,3},{5,4},{6,5},{7,6},{8,7},{9,8},{10,9},{11,1... | collective-permute-start | bytes 98312 | tf_op jit(solution)/shard_map/ppermute | solution.py:26
  289.1 5.1 collective-permute-start.11
  292.2 5.2 collective-permute-start.10
  431.1 9.5 %collective-permute-start.21 = (f32[1,64,128]{2,1,0:T(8,128)S(1)}, f32[1,64,128]{2,1,0:T(8,128)S(1)}, u32[]{:S(2)}, u32[]{:S(2)}) collective-permute-start(f32[1,64,128]{2,1,0:T(8,128)S(1)} %get-tuple-element.59), channel_id=1, source_target_pairs={{0,1},{1,2},{2,3},{3,4},{4,5},{5,6},{6,7},{7,8},{8,9},{9,10},{10,1... | collective-permute-start | bytes 98312 | tf_op jit(solution)/shard_map/ppermute | solution.py:25
  433.0 7.6 collective-permute-start.20
  435.4 5.1 collective-permute-start.13
  438.6 5.2 collective-permute-start.12
  576.4 136.0 %copy-start.4 = (s32[4,48]{1,0:T(4,128)S(1)}, s32[4,48]{1,0:T(4,128)}, u32[]{:S(2)}) copy-start(s32[4,48]{1,0:T(4,128)} %param.11) | copy-start | bytes 2308
  576.4 10.7 %collective-permute-start.23 = (f32[1,64,128]{2,1,0:T(8,128)S(1)}, f32[1,64,128]{2,1,0:T(8,128)S(1)}, u32[]{:S(2)}, u32[]{:S(2)}) collective-permute-start(f32[1,64,128]{2,1,0:T(8,128)S(1)} %get-tuple-element.55), channel_id=1, source_target_pairs={{0,1},{1,2},{2,3},{3,4},{4,5},{5,6},{6,7},{7,8},{8,9},{9,10},{10,1... | collective-permute-start | bytes 98312 | tf_op jit(solution)/shard_map/ppermute | solution.py:25
  578.3 8.8 %collective-permute-start.22 = (f32[1,64,128]{2,1,0:T(8,128)S(1)}, f32[1,64,128]{2,1,0:T(8,128)S(1)}, u32[]{:S(2)}, u32[]{:S(2)}) collective-permute-start(f32[1,64,128]{2,1,0:T(8,128)S(1)} %get-tuple-element.54), channel_id=1, source_target_pairs={{1,0},{2,1},{3,2},{4,3},{5,4},{6,5},{7,6},{8,7},{9,8},{10,9},{11,1... | collective-permute-start | bytes 98312 | tf_op jit(solution)/shard_map/ppermute | solution.py:26
  582.0 5.1 collective-permute-start.15
  585.2 5.2 collective-permute-start.14
  713.0 15.2 %collective-permute-start.24 = (f32[2,1,64,128]{3,2,1,0:T(8,128)S(1)}, f32[2,1,64,128]{3,2,1,0:T(8,128)S(1)}, u32[]{:S(2)}, u32[]{:S(2)}) collective-permute-start(f32[2,1,64,128]{3,2,1,0:T(8,128)S(1)} %get-tuple-element.51), channel_id=1, source_target_pairs={{1,0},{2,1},{3,2},{4,3},{5,4},{6,5},{7,6},{8,7},{9,8},{10,9},{11,1... | collective-permute-start | bytes 196616 | tf_op jit(solution)/shard_map/ppermute | solution.py:26
  725.2 4.3 collective-permute-start.25
  729.7 6.2 collective-permute-start.26
  731.6 5.6 collective-permute-start.27
  737.4 7.5 collective-permute-start.28
  739.3 5.6 collective-permute-start.29
  745.1 6.9 collective-permute-start.30
  747.0 5.6 collective-permute-start.31
Sparse Core Ops, SparseCore 0:
  55.7 73.5 all-gather.3
  654.1 57.3 all-gather.5
where the time goes:
time: 770 us; the launch traced here: 760 us
  blocking collectives  441 us (57%)
  waiting for transfers between devices  155 us (20%)
  starting transfers between devices  105 us (14%)
  between operations  33.6 us (4%)
  other arithmetic  18.4 us (2%)
    psum x4, blocking collectives, squares(): return lax.psum(jnp.sum(residual * residual), 'slab')  259 us
    psum x3, blocking collectives, conjugate(): curvature = lax.psum(jnp.sum(direction * applied), 'slab')  182 us
    all_gather x1, waiting for transfers between devices, body(): gathered = lax.all_gather(offered[None], 'sec', axis=0, tiled=True)  73 us
    ppermute x16, starting transfers between devices, extended(): before = lax.ppermute(last, axis, up)  57.5 us
    all_gather x1, waiting for transfers between devices, body(): returned_rows = lax.all_gather(sensitivity[None], 'sec', axis=0, tiled=True)  57.5 us
    ppermute x16, starting transfers between devices, extended(): after = lax.ppermute(first, axis, down)  47.6 us
    ppermute x16, waiting for transfers between devices, extended(): after = lax.ppermute(first, axis, down)  21.5 us
  transfers between devices with their start and end apart: 34, of which 12 were waited for; matrix products, arithmetic and copies ran while one was open for 1% of the time, Pallas kernels for 0%

commit v1 on v0

v1 whole, which is shorter than its diff:
```python
import functools
import math

import jax
import jax.numpy as jnp
from jax import lax
from jax.experimental import pallas as pl
from jax.experimental.pallas import tpu as pltpu
from jax.sharding import PartitionSpec as P

STEPS = 4
PAIRCAP = 8
BASIS = 4

time_step = 0.1
sink_rate = 0.5
period_steps = 16.0

CENTRE = 6.8
RADIUS = 6.4

MESH = pl.DeviceIdType.MESH
HIGHEST = lax.Precision.HIGHEST


def in_plane(c):
    rows, cols = c.shape
    row = lax.broadcasted_iota(jnp.int32, c.shape, 0)
    col = lax.broadcasted_iota(jnp.int32, c.shape, 1)
    up = jnp.where(row == 0, 0.0, pltpu.roll(c, 1, 0))
    down = jnp.where(row == rows - 1, 0.0, pltpu.roll(c, rows - 1, 0))
    left = jnp.where(col == 0, 0.0, pltpu.roll(c, 1, 1))
    right = jnp.where(col == cols - 1, 0.0, pltpu.roll(c, cols - 1, 1))
    return (up + down) + (left + right)


def fold(values):
    rows, cols = values.shape
    return jnp.sum(values.reshape(rows // 8, 8, cols), axis=0)


def coefficients(sums):
    total = jnp.broadcast_to(jnp.sum(sums, axis=1, keepdims=True), sums.shape)
    s = [total[k : k + 1, :] for k in range(8)]
    nu = [s[0], s[1], 2.0 * s[2] - s[0], 2.0 * s[3] - s[1], 2.0 * s[4] - s[0], 2.0 * s[5] - s[1], 2.0 * s[6] - s[0]]
    nu.append(4.0 * s[7] - 2.0 * s[5] - s[1])
    shift = 2.0 * CENTRE / RADIUS
    u = [shift * nu[k] + nu[k + 1] + nu[abs(k - 1)] for k in range(7)]
    mat = [[u[i + j] + u[abs(i - j)] for j in range(BASIS)] for i in range(BASIS)]
    diag = [mat[i][i] for i in range(BASIS)]
    rhs = [(4.0 / RADIUS) * nu[i] for i in range(BASIS)]
    inverse = []
    for k in range(BASIS):
        good = mat[k][k] > 1e-8 * diag[k]
        inv = jnp.where(good, 1.0 / jnp.where(good, mat[k][k], 1.0), 0.0)
        inverse.append(inv)
        for i in range(k + 1, BASIS):
            factor = mat[k][i] * inv
            for j in range(i, BASIS):
                mat[i][j] = mat[i][j] - factor * mat[k][j]
            rhs[i] = rhs[i] - factor * rhs[k]
    out = [None] * BASIS
    for i in reversed(range(BASIS)):
        value = rhs[i]
        for j in range(i + 1, BASIS):
            value = value - mat[i][j] * out[j]
        out[i] = value * inverse[i]
    return out


def kernel(
    n_sec,
    n_slab,
    group,
    part_ref,
    line_ref,
    flag_ref,
    instant_ref,
    heat_ref,
    factor_ref,
    dual_ref,
    state_ref,
    adjoint_ref,
    heat,
    coef,
    dual,
    a1,
    a2,
    a3,
    own,
    keep,
    mu_a,
    mu_b,
    w_a,
    w_b,
    pick,
    offered,
    slots,
    placed,
    back,
    returned,
    tile_a,
    tile_b,
    gather_a,
    gather_b,
    result,
    local_sem,
    out_sem,
    halo_send,
    halo_recv,
    row_send,
    row_recv,
    side_send,
    side_recv,
    sum_send_a,
    sum_send_b,
    sum_recv,
):
    ingots, contact = part_ref.shape
    melts = n_sec - ingots
    depth, height, width = heat_ref.shape
    first, last = depth, 2 * depth
    second = n_slab // group
    sec, slab = lax.axis_index("sec"), lax.axis_index("slab")
    is_melt = sec < melts
    has_left, has_right = slab > 0, slab < n_slab - 1
    low = jnp.where(has_left, 0, first)
    high = jnp.where(has_right, 3 * depth, last)

    loads = [
        pltpu.make_async_copy(src, dst.at[pl.ds(first, depth)], local_sem.at[i])
        for i, (src, dst) in enumerate(((heat_ref, heat), (factor_ref, coef), (dual_ref, dual)))
    ]
    for load in loads:
        load.start()

    barrier = pltpu.get_barrier_semaphore()

    def greet(to_sec, to_slab):
        pl.semaphore_signal(barrier, inc=1, device_id=(to_sec, to_slab), device_id_type=MESH)

    pl.when(has_left)(lambda: greet(sec, slab - 1))
    pl.when(has_right)(lambda: greet(sec, slab + 1))
    base = (slab // group) * group

    def peer_a(offset):
        return base + lax.rem(slab - base + offset, group)

    def peer_b(offset):
        return lax.rem(slab + offset * group, n_slab)

    beside = has_left.astype(jnp.int32) + has_right.astype(jnp.int32)

    @pl.when(is_melt)
    def _():
        for j in range(ingots):
            greet(melts + j, slab)

    @pl.when(jnp.logical_not(is_melt))
    def _():
        for m in range(melts):
            greet(m, slab)
        for offset in range(1, group):
            greet(sec, peer_a(offset))
        for offset in range(1, second):
            greet(sec, peer_b(offset))

    pl.semaphore_wait(barrier, beside + jnp.where(is_melt, ingots, melts + group - 1 + second - 1))

    def halo(src, dst, send, recv, lefts, rights):
        (left_src, left_dst), (right_src, right_dst) = lefts, rights
        to_left = pltpu.make_async_remote_copy(
            src_ref=src.at[left_src], dst_ref=dst.at[left_dst], send_sem=send.at[0], recv_sem=recv.at[1],
            device_id=(sec, slab - 1), device_id_type=MESH,
        )
        to_right = pltpu.make_async_remote_copy(
            src_ref=src.at[right_src], dst_ref=dst.at[right_dst], send_sem=send.at[1], recv_sem=recv.at[0],
            device_id=(sec, slab + 1), device_id_type=MESH,
        )
        return to_left, to_right

    def start(pair):
        pl.when(has_left)(lambda: pair[0].start())
        pl.when(has_right)(lambda: pair[1].start())

    def wait_recv(pair):
        pl.when(has_right)(lambda: pair[0].wait_recv())
        pl.when(has_left)(lambda: pair[1].wait_recv())

    def wait_send(pair):
        pl.when(has_left)(lambda: pair[0].wait_send())
        pl.when(has_right)(lambda: pair[1].wait_send())

    whole = (pl.ds(0, depth), pl.ds(last, depth)), (pl.ds(0, depth), pl.ds(0, depth))
    heat_halo = halo(heat_ref, heat, halo_send.at[0], halo_recv.at[0], *whole)
    coef_halo = halo(factor_ref, coef, halo_send.at[1], halo_recv.at[1], *whole)
    dual_halo = halo(dual_ref, dual, halo_send.at[2], halo_recv.at[2], *whole)

    zero = jnp.zeros((height, width), jnp.float32)

    def clear(bufs):
        @pl.when(jnp.logical_not(has_left))
        def _():
            for buf in bufs:
                buf[first - 1] = zero

        @pl.when(jnp.logical_not(has_right))
        def _():
            for buf in bufs:
                buf[last] = zero

    row_i = lax.broadcasted_iota(jnp.int32, (contact, contact), 0)
    lane_i = lax.broadcasted_iota(jnp.int32, (contact, contact), 1)

    def column(row):
        return jnp.sum(jnp.where(row_i == lane_i, row, 0.0), axis=1, keepdims=True)

    @pl.when(is_melt)
    def _():
        start(heat_halo)
        start(coef_halo)
        clear((heat, a1, a2, a3, dual, mu_a, mu_b, w_a, w_b))

        for j in range(ingots):
            named = part_ref[j : j + 1, :].astype(jnp.float32) == sec.astype(jnp.float32)
            lines = line_ref[j : j + 1, :].astype(jnp.float32)
            before = column(jnp.where(named, 1.0, 0.0))
            rank = jnp.sum(jnp.where(row_i < lane_i, before, 0.0), axis=0, keepdims=True)
            slot = lax.broadcasted_iota(jnp.int32, (PAIRCAP, contact), 0).astype(jnp.float32)
            chosen = jnp.where(named, 1.0, 0.0) * jnp.where(rank == slot, 1.0, 0.0)
            slot_line = jnp.sum(chosen * lines, axis=1, keepdims=True)
            live = jnp.sum(chosen, axis=1, keepdims=True)
            q = lax.broadcasted_iota(jnp.int32, (PAIRCAP, height), 1).astype(jnp.float32)
            pick[pl.ds(j * PAIRCAP, PAIRCAP), :] = jnp.where(q == slot_line, live, 0.0)

        archived = instant_ref[0].astype(jnp.float32)
        speeds = []
        for k in range(STEPS):
            phase = jnp.full((1, width), archived + k)
            speeds.append(1.0 + 0.5 * jnp.sin(2.0 * math.pi * phase / period_steps))

        for load in loads:
            load.wait()
        wait_recv(heat_halo)
        wait_recv(coef_halo)
        start(dual_halo)

        states = (heat, a1, a2, a3, own)
        for k in range(STEPS):
            src, dst = states[k], states[k + 1]
            shift = first if k == STEPS - 1 else 0

            def forward(z, carry, k=k, src=src, dst=dst, shift=shift):
                c = src[z]
                below = src[z - 1]
                total = (below + src[z + 1]) + in_plane(c)
                change = coef[z] * (total - 6.0 * c) - speeds[k] * (c - below)
                bent = jnp.tanh(c)
                dst[z - shift] = c + time_step * change - time_step * sink_rate * bent
                keep[k, z] = 1.0 - time_step * sink_rate * (1.0 - bent * bent)
                return carry

            lax.fori_loop(jnp.maximum(low, 1 + k), jnp.minimum(high, 3 * depth - 1 - k), forward, 0)

        keep3 = keep.at[3]
        keep_halo = halo(
            keep3, keep3, side_send.at[0], side_recv.at[0],
            (pl.ds(first, depth - 1), pl.ds(last, depth - 1)), (pl.ds(first + 1, depth - 1), pl.ds(1, depth - 1)),
        )
        start(keep_halo)
        for z in range(depth):
            offered[z] = jnp.dot(pick[...], own[z], precision=HIGHEST, preferred_element_type=jnp.float32)
        sends = []
        for j in range(ingots):
            send = pltpu.make_async_remote_copy(
                src_ref=offered.at[:, pl.ds(j * PAIRCAP, PAIRCAP), :],
                dst_ref=slots.at[:, pl.ds(pl.multiple_of(sec * PAIRCAP, PAIRCAP), PAIRCAP), :],
                send_sem=row_send.at[j], recv_sem=row_recv, device_id=(melts + j, slab), device_id_type=MESH,
            )
            send.start()
            sends.append(send)
        state_out = pltpu.make_async_copy(own, state_ref, out_sem.at[0])
        state_out.start()

        for z in (first - 2, last + 1):
            bent = jnp.tanh(a2[z])
            keep[2, z] = 1.0 - time_step * sink_rate * (1.0 - bent * bent)
        wait_recv(dual_halo)
        wait_recv(keep_halo)

        here = returned.at[pl.ds(first, depth)]
        pltpu.make_async_copy(here, here, row_recv).wait()
        back_halo = halo(
            returned, returned, side_send.at[1], side_recv.at[1],
            (pl.ds(first, depth), pl.ds(last, depth)), (pl.ds(first, depth), pl.ds(0, depth)),
        )
        start(back_halo)

        def add_returned(z, carry):
            rows = lax.dot_general(
                pick[...], returned[z], (((0,), (0,)), ((), ())), precision=HIGHEST, preferred_element_type=jnp.float32
            )
            value = dual[z] + rows
            dual[z] = value
            w_a[z] = coef[z] * value
            return carry

        lax.fori_loop(first, last, add_returned, 0)
        wait_recv(back_halo)
        lax.fori_loop(low, first, add_returned, 0)
        lax.fori_loop(last, high, add_returned, 0)

        mus = (result, mu_b, mu_a, mu_b, dual)
        ws = (None, w_b, w_a, w_b, w_a)
        for k in reversed(range(STEPS)):
            src, dst, wsrc, wdst = mus[k + 1], mus[k], ws[k + 1], ws[k]
            shift = first if k == 0 else 0

            def backward(z, carry, k=k, src=src, dst=dst, wsrc=wsrc, wdst=wdst, shift=shift):
                c, w = src[z], wsrc[z]
                total = (wsrc[z - 1] + wsrc[z + 1]) + in_plane(w)
                change = total - 6.0 * w - speeds[k] * (c - src[z + 1])
                value = keep[k, z] * c + time_step * change
                dst[z - shift] = value
                if wdst is not None:
                    wdst[z] = coef[z] * value
                return carry

            lax.fori_loop(jnp.maximum(low, first - k), jnp.minimum(high, last + k), backward, 0)

        adjoint_out = pltpu.make_async_copy(result, adjoint_ref, out_sem.at[1])
        adjoint_out.start()
        for pair in (heat_halo, coef_halo, dual_halo, keep_halo, back_halo):
            wait_send(pair)
        for send in sends:
            send.wait_send()
        state_out.wait()
        adjoint_out.wait()

    @pl.when(jnp.logical_not(is_melt))
    def _():
        start(dual_halo)
        start(coef_halo)
        clear((heat, dual, a1, a2, a3))

        mine = sec - melts
        names = part_ref[pl.ds(mine, 1), :].astype(jnp.float32)
        flags = flag_ref[pl.ds(mine, 1), :].astype(jnp.float32)
        names_col, flags_col = column(names), column(flags)
        same = jnp.where(names_col == names, 1.0, 0.0)
        rank_col = jnp.sum(jnp.where(lane_i < row_i, same, 0.0), axis=1, keepdims=True)
        rank_row = jnp.sum(jnp.where(row_i < lane_i, same, 0.0), axis=0, keepdims=True)
        count = melts * PAIRCAP
        slot_lane = lax.broadcasted_iota(jnp.int32, (contact, count), 1).astype(jnp.float32)
        slot_row = lax.broadcasted_iota(jnp.int32, (count, contact), 0).astype(jnp.float32)
        place = jnp.where(slot_lane == names_col * PAIRCAP + rank_col, flags_col, 0.0)
        give = jnp.where(slot_row == names * PAIRCAP + rank_row, flags, 0.0)

        for load in loads:
            load.wait()
        wait_recv(dual_halo)
        wait_recv(coef_halo)
        start(heat_halo)

        pending = []

        def solve(which, t0, out):
            ts = (t0, a1, a2, a3)

            def image(t, z):
                c = t[z]
                return (coef[z] - (CENTRE - 6.0)) * c - ((t[z - 1] + t[z + 1]) + in_plane(c))

            for k in range(1, BASIS):

                def grow(z, carry, k=k):
                    value = image(ts[k - 1], z)
                    if k == 1:
                        ts[k][z] = value * (1.0 / RADIUS)
                    else:
                        ts[k][z] = value * (2.0 / RADIUS) - ts[k - 2][z]
                    return carry

                reach = BASIS - 1 - k
                lax.fori_loop(jnp.maximum(low, first - reach), jnp.minimum(high, last + 1 + reach), grow, 0)

            def dots(z, sums):
                t = [ref[z] for ref in ts]
                image3 = (coef[z] - (CENTRE - 6.0)) * t[3] - 2.0 * a3[z + 1] - in_plane(t[3])
                terms = (
                    t[0] * t[0], t[0] * t[1], t[1] * t[1], t[1] * t[2],
                    t[2] * t[2], t[2] * t[3], t[3] * t[3], t[3] * image3 * (1.0 / RADIUS),
                )
                return tuple(s + fold(term) for s, term in zip(sums, terms))

            sums = lax.fori_loop(first, last, dots, (jnp.zeros((8, width), jnp.float32),) * 8)
            for k in range(8):
                tile_a[which, pl.ds(k, 1), :] = jnp.sum(sums[k], axis=0, keepdims=True)

            def exchange(tile, gather, send_sem, recv_sem, size, peer):
                for offset in range(1, size):
                    copy = pltpu.make_async_remote_copy(
                        src_ref=tile.at[which], dst_ref=gather.at[which, offset - 1],
                        send_sem=send_sem.at[which, offset - 1], recv_sem=recv_sem,
                        device_id=(sec, peer(offset)), device_id_type=MESH,
                    )
                    copy.start()
                    pending.append(copy)
                if size > 1:
                    pltpu.make_async_copy(gather.at[which], gather.at[which], recv_sem).wait()
                total = tile[which]
                for offset in range(1, size):
                    total = total + gather[which, offset - 1]
                return total

            tile_b[which] = exchange(tile_a, gather_a, sum_send_a, sum_recv.at[which, 0], group, peer_a)
            total = exchange(tile_b, gather_b, sum_send_b, sum_recv.at[which, 1], second, peer_b)
            c = coefficients(total)

            def combine(z, carry):
                out[z - first] = (c[0] * ts[0][z] + c[1] * ts[1][z]) + (c[2] * ts[2][z] + c[3] * ts[3][z])
                return carry

            lax.fori_loop(first, last, combine, 0)

        solve(0, dual, own)
        for z in range(depth):
            back[z] = jnp.dot(give, own[z, :contact, :], precision=HIGHEST, preferred_element_type=jnp.float32)
        sends = []
        for m in range(melts):
            send = pltpu.make_async_remote_copy(
                src_ref=back.at[:, pl.ds(m * PAIRCAP, PAIRCAP), :],
                dst_ref=returned.at[pl.ds(first, depth), pl.ds(pl.multiple_of(mine * PAIRCAP, PAIRCAP), PAIRCAP), :],
                send_sem=row_send.at[m], recv_sem=row_recv, device_id=(m, slab), device_id_type=MESH,
            )
            send.start()
            sends.append(send)
        adjoint_out = pltpu.make_async_copy(own, adjoint_ref, out_sem.at[1])
        adjoint_out.start()

        pltpu.make_async_copy(slots, slots, row_recv).wait()
        for z in range(depth):
            placed[first + z] = jnp.dot(place, slots[z], precision=HIGHEST, preferred_element_type=jnp.float32)
        placed_halo = halo(
            placed, placed, side_send.at[0], side_recv.at[0],
            (pl.ds(first, depth), pl.ds(last, depth)), (pl.ds(first, depth), pl.ds(0, depth)),
        )
        start(placed_halo)
        wait_recv(heat_halo)
        wait_recv(placed_halo)

        def load_up(z, carry):
            heat[z, pl.ds(0, contact), :] = heat[z, pl.ds(0, contact), :] + placed[z]
            return carry

        lax.fori_loop(low, high, load_up, 0)
        solve(1, heat, result)
        state_out = pltpu.make_async_copy(result, state_ref, out_sem.at[0])
        state_out.start()

        for pair in (heat_halo, coef_halo, dual_halo, placed_halo):
            wait_send(pair)
        for copy in sends + pending:
            copy.wait_send()
        state_out.wait()
        adjoint_out.wait()


def body(n_sec, n_slab, group, heat_level, material_factor, dual_sensitivity, part, line, flag, instant):
    ingots, contact = line.shape
    melts = n_sec - ingots
    _, depth, height, width = heat_level.shape
    second = n_slab // group
    f32 = jnp.float32
    wide = pltpu.VMEM((3 * depth, height, width), f32)
    slab_buf = pltpu.VMEM((depth, height, width), f32)
    dma = pltpu.SemaphoreType.DMA
    scratch = [
        wide, wide, wide, wide, wide, wide, slab_buf,
        pltpu.VMEM((STEPS, 3 * depth, height, width), f32),
        wide, wide, wide, wide,
        pltpu.VMEM((ingots * PAIRCAP, height), f32),
        pltpu.VMEM((depth, ingots * PAIRCAP, width), f32),
        pltpu.VMEM((depth, melts * PAIRCAP, width), f32),
        pltpu.VMEM((3 * depth, contact, width), f32),
        pltpu.VMEM((depth, melts * PAIRCAP, width), f32),
        pltpu.VMEM((3 * depth, ingots * PAIRCAP, width), f32),
        pltpu.VMEM((2, 8, width), f32),
        pltpu.VMEM((2, 8, width), f32),
        pltpu.VMEM((2, max(group - 1, 1), 8, width), f32),
        pltpu.VMEM((2, max(second - 1, 1), 8, width), f32),
        slab_buf,
        dma((3,)), dma((2,)), dma((3, 2)), dma((3, 2)),
        dma((max(melts, ingots),)), dma, dma((2, 2)), dma((2, 2)),
        dma((2, max(group - 1, 1))), dma((2, max(second - 1, 1))), dma((2, 2)),
    ]
    vmem, smem, anywhere = (pl.BlockSpec(memory_space=s) for s in (pltpu.VMEM, pltpu.SMEM, pl.ANY))
    shape = jax.ShapeDtypeStruct((depth, height, width), f32)
    state, adjoint = pl.pallas_call(
        functools.partial(kernel, n_sec, n_slab, group),
        out_shape=(shape, shape),
        in_specs=[vmem, vmem, vmem, smem, anywhere, anywhere, anywhere],
        out_specs=(anywhere, anywhere),
        scratch_shapes=scratch,
        compiler_params=pltpu.CompilerParams(
            collective_id=0, has_side_effects=True, vmem_limit_bytes=32 * 1024 * 1024
        ),
    )(part[:, :, 0], line, flag, instant, heat_level[0], material_factor[0], dual_sensitivity[0])
    return state[None], adjoint[None]


def solution(mesh):
    n_sec, n_slab = mesh.shape["sec"], mesh.shape["slab"]
    group = min(8, max(1, n_slab // 2))
    fields = P("sec", "slab", None, None)
    return jax.shard_map(
        functools.partial(body, n_sec, n_slab, group),
        mesh=mesh,
        in_specs=(fields, fields, fields, P(), P(), P(), P()),
        out_specs=(fields, fields),
        check_vma=False,
    )
```

time: 770 us -> 54.7 us (0.07); the launches traced: 760 us -> 54.5 us
  blocking collectives: 441 us -> 0 us
  waiting for transfers between devices: 155 us -> 0 us
  starting transfers between devices: 105 us -> 0 us
  Pallas kernels: 0 us -> 48.5 us
  between operations: 33.6 us -> 1.32 us
  other arithmetic: 18.4 us -> 0 us
    psum x7 -> x0, blocking collectives: 441 us -> none  [the longest x4 259 us: squares(): return lax.psum(jnp.sum(residual * residual), 'slab')]
    all_gather x2 -> x0, waiting for transfers between devices: 130 us -> none  [the longest x1 73 us: body(): gathered = lax.all_gather(offered[None], 'sec', axis=0, tiled=True)]
    ppermute x32 -> x0, starting transfers between devices: 105 us -> none  [the longest x16 57.5 us: extended(): before = lax.ppermute(last, axis, up)]
    pallas_call x0 -> x1, Pallas kernels: none -> 48.5 us  [body(): pl.pallas_call(functools.partial(kernel, n_sec, n_slab, group), out_shape...]
    ppermute x32 -> x0, waiting for transfers between devices: 24.8 us -> none  [the longest x16 21.5 us: extended(): after = lax.ppermute(first, axis, down)]
    reduce_sum x12 -> x0, other arithmetic: 11 us -> none  [the longest x5 5.86 us: conjugate(): curvature = lax.psum(jnp.sum(direction * applied), 'slab')]
  transfers between devices with their start and end apart: 34 -> 0, of which waited for: 12 -> 0; matrix products, arithmetic and copies ran while one was open for 1% -> 0% of each run, Pallas kernels for 0% -> 0%
where the time goes in v1:
time: 54.7 us; the launch traced here: 54.5 us
  Pallas kernels  48.5 us (89%)
  local copies, waits for them, and re-layouts  4.71 us (9%)
  between operations  1.32 us (2%)
    pallas_call x1, Pallas kernels, body(): pl.pallas_call(functools.partial(kernel, n_sec, n_slab, group), out_shape...  48.5 us
    unnamed x14, local copies, waits for them, and re-layouts  4.71 us

profile of v1, /device:TPU:1, one launch (start us, length us, event | category | flops | bytes accessed | tf_op | source)
XLA Modules:
  0.0 54.5 jit_solution(1846229754335971852)
XLA Ops:
  1.3 0.0 copy-start.5
  1.3 0.0 copy-start.4
  1.3 0.0 copy-start.3
  1.3 0.7 %copy-done.5 = s32[4,48]{1,0:T(4,128)S(1)} copy-done((s32[4,48]{1,0:T(4,128)S(1)}, s32[4,48]{1,0:T(4,128)}, u32[]{:S(2)}) %copy-start.5) | copy-done | bytes 792
  2.0 0.0 copy-done.4
  2.0 0.0 copy-done.3
  2.0 0.0 copy-start
  2.0 0.9 %copy-done = f32[1,4,64,128]{3,2,1,0:T(8,128)S(1)} copy-done((f32[1,4,64,128]{3,2,1,0:T(8,128)S(1)}, f32[1,4,64,128]{3,2,1,0:T(8,128)}, u32[]{:S(2)}) %copy-start) | copy-done | bytes 131096
  2.9 0.0 copy-start.1
  2.9 0.9 %copy-done.1 = f32[1,4,64,128]{3,2,1,0:T(8,128)S(1)} copy-done((f32[1,4,64,128]{3,2,1,0:T(8,128)S(1)}, f32[1,4,64,128]{3,2,1,0:T(8,128)}, u32[]{:S(2)}) %copy-start.1) | copy-done | bytes 131096
  3.8 0.0 copy-start.2
  3.8 0.9 %copy-done.2 = f32[1,4,64,128]{3,2,1,0:T(8,128)S(1)} copy-done((f32[1,4,64,128]{3,2,1,0:T(8,128)S(1)}, f32[1,4,64,128]{3,2,1,0:T(8,128)}, u32[]{:S(2)}) %copy-start.2) | copy-done | bytes 131096
  4.7 48.5 %shard_map.86 = (f32[4,64,128]{2,1,0:T(8,128)S(1)}, f32[4,64,128]{2,1,0:T(8,128)S(1)}) custom-call(s32[4,48]{1,0:T(4,128)S(1)} %bitcast.11, s32[4,48]{1,0:T(4,128)S(1)} %copy-done.4, s32[4,48]{1,0:T(4,128)S(1)} %copy-done.5, s32[1]{0:T(128)S(6)} %copy.11.instant_ref, f32[4,64,128]{2,1,0:T(8,128)S(1)} %bitcast.6, f32[4,64,128]{2,1,0:T(8,128)S(1)} %bitcast.7, ...), custom_call_target="tpu_custom_call" | custom-call | tf_op jit(solution)/shard_map/pallas_call | solution.py:499
  53.2 0.7 %copy.12 = f32[1,4,64,128]{3,2,1,0:T(8,128)} copy(f32[1,4,64,128]{3,2,1,0:T(8,128)S(1)} %bitcast.10) | data formatting | bytes 262144
  53.9 0.7 %copy.13 = f32[1,4,64,128]{3,2,1,0:T(8,128)} copy(f32[1,4,64,128]{3,2,1,0:T(8,128)S(1)} %bitcast.9) | data formatting | bytes 262144
Async XLA Ops:
  1.3 0.7 %copy-start.5 = (s32[4,48]{1,0:T(4,128)S(1)}, s32[4,48]{1,0:T(4,128)}, u32[]{:S(2)}) copy-start(s32[4,48]{1,0:T(4,128)} %flag_ref.1) | copy-start | bytes 2308
  1.3 0.7 %copy-start.4 = (s32[4,48]{1,0:T(4,128)S(1)}, s32[4,48]{1,0:T(4,128)}, u32[]{:S(2)}) copy-start(s32[4,48]{1,0:T(4,128)} %line_ref.1) | copy-start | bytes 2308
  1.3 0.7 %copy-start.3 = (s32[4,48,1]{1,2,0:T(1,128)S(1)}, s32[4,48,1]{1,2,0:T(1,128)}, u32[]{:S(2)}) copy-start(s32[4,48,1]{1,2,0:T(1,128)} %param.10) | copy-start | bytes 2308
  2.0 0.9 %copy-start = (f32[1,4,64,128]{3,2,1,0:T(8,128)S(1)}, f32[1,4,64,128]{3,2,1,0:T(8,128)}, u32[]{:S(2)}) copy-start(f32[1,4,64,128]{3,2,1,0:T(8,128)} %param.7) | copy-start | bytes 393220
  2.9 0.9 %copy-start.1 = (f32[1,4,64,128]{3,2,1,0:T(8,128)S(1)}, f32[1,4,64,128]{3,2,1,0:T(8,128)}, u32[]{:S(2)}) copy-start(f32[1,4,64,128]{3,2,1,0:T(8,128)} %param.8) | copy-start | bytes 393220
  3.8 0.9 %copy-start.2 = (f32[1,4,64,128]{3,2,1,0:T(8,128)S(1)}, f32[1,4,64,128]{3,2,1,0:T(8,128)}, u32[]{:S(2)}) copy-start(f32[1,4,64,128]{3,2,1,0:T(8,128)} %param.9) | copy-start | bytes 393220

commit v2 on v1

--- a/solution.py
+++ b/solution.py
@@ -72,15 +72,19 @@
     n_sec,
     n_slab,
     group,
-    part_ref,
-    line_ref,
-    flag_ref,
-    instant_ref,
+    part_hbm,
+    line_hbm,
+    flag_hbm,
+    instant_hbm,
     heat_ref,
     factor_ref,
     dual_ref,
     state_ref,
     adjoint_ref,
+    part_ref,
+    line_ref,
+    flag_ref,
+    instant_ref,
     heat,
     coef,
     dual,
@@ -116,7 +120,7 @@
     sum_send_b,
     sum_recv,
 ):
-    ingots, contact = part_ref.shape
+    ingots, contact = part_hbm.shape
     melts = n_sec - ingots
     depth, height, width = heat_ref.shape
     first, last = depth, 2 * depth
@@ -131,7 +135,13 @@
         pltpu.make_async_copy(src, dst.at[pl.ds(first, depth)], local_sem.at[i])
         for i, (src, dst) in enumerate(((heat_ref, heat), (factor_ref, coef), (dual_ref, dual)))
     ]
-    for load in loads:
+    tables = [
+        pltpu.make_async_copy(src, dst, local_sem.at[3 + i])
+        for i, (src, dst) in enumerate(
+            ((part_hbm, part_ref), (line_hbm, line_ref), (flag_hbm, flag_ref), (instant_hbm, instant_ref))
+        )
+    ]
+    for load in tables + loads:
         load.start()
 
     barrier = pltpu.get_barrier_semaphore()
@@ -209,6 +219,8 @@
             for buf in bufs:
                 buf[last] = zero
 
+    for load in tables:
+        load.wait()
     row_i = lax.broadcasted_iota(jnp.int32, (contact, contact), 0)
     lane_i = lax.broadcasted_iota(jnp.int32, (contact, contact), 1)
 
@@ -476,6 +488,8 @@
     slab_buf = pltpu.VMEM((depth, height, width), f32)
     dma = pltpu.SemaphoreType.DMA
     scratch = [
+        pltpu.VMEM((ingots, contact), jnp.int32), pltpu.VMEM((ingots, contact), jnp.int32),
+        pltpu.VMEM((ingots, contact), jnp.int32), pltpu.SMEM((1,), jnp.int32),
         wide, wide, wide, wide, wide, wide, slab_buf,
         pltpu.VMEM((STEPS, 3 * depth, height, width), f32),
         wide, wide, wide, wide,
@@ -490,20 +504,20 @@
         pltpu.VMEM((2, max(group - 1, 1), 8, width), f32),
         pltpu.VMEM((2, max(second - 1, 1), 8, width), f32),
         slab_buf,
-        dma((3,)), dma((2,)), dma((3, 2)), dma((3, 2)),
+        dma((7,)), dma((2,)), dma((3, 2)), dma((3, 2)),
         dma((max(melts, ingots),)), dma, dma((2, 2)), dma((2, 2)),
         dma((2, max(group - 1, 1))), dma((2, max(second - 1, 1))), dma((2, 2)),
     ]
-    vmem, smem, anywhere = (pl.BlockSpec(memory_space=s) for s in (pltpu.VMEM, pltpu.SMEM, pl.ANY))
+    hbm = pl.BlockSpec(memory_space=pltpu.HBM)
     shape = jax.ShapeDtypeStruct((depth, height, width), f32)
     state, adjoint = pl.pallas_call(
         functools.partial(kernel, n_sec, n_slab, group),
         out_shape=(shape, shape),
-        in_specs=[vmem, vmem, vmem, smem, anywhere, anywhere, anywhere],
-        out_specs=(anywhere, anywhere),
+        in_specs=[hbm] * 7,
+        out_specs=(hbm, hbm),
         scratch_shapes=scratch,
         compiler_params=pltpu.CompilerParams(
-            collective_id=0, has_side_effects=True, vmem_limit_bytes=32 * 1024 * 1024
+            collective_id=0, has_side_effects=True, vmem_limit_bytes=60 * 1024 * 1024
         ),
     )(part[:, :, 0], line, flag, instant, heat_level[0], material_factor[0], dual_sensitivity[0])
     return state[None], adjoint[None]

time: 54.7 us -> 52.4 us (0.958)
  local copies, waits for them, and re-layouts: 4.71 us -> 2.26 us
    unnamed x14 -> x4, local copies, waits for them, and re-layouts: 4.71 us -> 2.26 us
where the time goes in v2:
time: 52.4 us; the launch traced here: 52.3 us
  Pallas kernels  48.7 us (93%)
  local copies, waits for them, and re-layouts  2.26 us (4%)
  between operations  1.3 us (2%)
    pallas_call x1, Pallas kernels, body(): pl.pallas_call(functools.partial(kernel, n_sec, n_slab, group), out_shape...  48.7 us
    unnamed x4, local copies, waits for them, and re-layouts  2.26 us

profile of v2, /device:TPU:1, one launch (start us, length us, event | category | flops | bytes accessed | tf_op | source)
XLA Modules:
  0.0 52.3 jit_solution(12924802112911743319)
XLA Ops:
  1.3 48.7 %shard_map.86 = (f32[4,64,128]{2,1,0:T(8,128)}, f32[4,64,128]{2,1,0:T(8,128)}) custom-call(s32[4,48]{1,0:T(4,128)} %bitcast.11, s32[4,48]{1,0:T(4,128)} %line_hbm.1, s32[4,48]{1,0:T(4,128)} %flag_hbm.1, s32[1]{0:T(128)S(6)} %copy.11.instant_hbm, f32[4,64,128]{2,1,0:T(8,128)} %bitcast.6, f32[4,64,128]{2,1,0:T(8,128)} %bitcast.7, f32[4,64,128]{2,1,0:T(8,128)} %bitcast.8), custom_call_target="tpu_custom_call" | custom-call | tf_op jit(solution)/shard_map/pallas_call | solution.py:513
  50.0 0.0 copy-start
  50.0 1.6 %copy.12 = f32[1,4,64,128]{3,2,1,0:T(8,128)} copy(f32[1,4,64,128]{3,2,1,0:T(8,128)} %bitcast.10) | data formatting | bytes 262144
  51.6 0.0 copy-done
  51.6 0.7 %copy.13 = f32[1,4,64,128]{3,2,1,0:T(8,128)} copy(f32[1,4,64,128]{3,2,1,0:T(8,128)S(1)} %bitcast.9) | data formatting | bytes 262144
Async XLA Ops:
  50.0 1.6 %copy-start = (f32[4,64,128]{2,1,0:T(8,128)S(1)}, f32[4,64,128]{2,1,0:T(8,128)}, u32[]{:S(2)}) copy-start(f32[4,64,128]{2,1,0:T(8,128)} %get-tuple-element.5) | copy-start | bytes 393220

commit v3 on v2

v3 whole, which is shorter than its diff:
```python
import functools
import math

import jax
import jax.numpy as jnp
from jax import lax
from jax.experimental import pallas as pl
from jax.experimental.pallas import tpu as pltpu
from jax.sharding import PartitionSpec as P

STEPS = 4
PAIRCAP = 8
BASIS = 4

time_step = 0.1
sink_rate = 0.5
period_steps = 16.0

CENTRE = 6.8
RADIUS = 6.4

MESH = pl.DeviceIdType.MESH
HIGHEST = lax.Precision.HIGHEST


def in_plane(c):
    rows, cols = c.shape
    row = lax.broadcasted_iota(jnp.int32, c.shape, 0)
    col = lax.broadcasted_iota(jnp.int32, c.shape, 1)
    up = jnp.where(row == 0, 0.0, pltpu.roll(c, 1, 0))
    down = jnp.where(row == rows - 1, 0.0, pltpu.roll(c, rows - 1, 0))
    left = jnp.where(col == 0, 0.0, pltpu.roll(c, 1, 1))
    right = jnp.where(col == cols - 1, 0.0, pltpu.roll(c, cols - 1, 1))
    return (up + down) + (left + right)


def fold(values):
    rows, cols = values.shape
    return jnp.sum(values.reshape(rows // 8, 8, cols), axis=0)


def own_lanes(values):
    row = lax.broadcasted_iota(jnp.int32, values.shape, 0)
    lane = lax.broadcasted_iota(jnp.int32, values.shape, 1)
    each = values.shape[1] // values.shape[0]
    return jnp.where((lane >= row * each) & (lane < (row + 1) * each), values, 0.0)


def pack(values):
    lanes = values.shape[1]
    for distance in (lanes // 2, lanes // 4, lanes // 8):
        values = values + pltpu.roll(values, distance, 1)
    return jnp.sum(own_lanes(values), axis=0, keepdims=True)


def coefficients(packed):
    spread = own_lanes(jnp.broadcast_to(packed, (8, packed.shape[1])))
    total = jnp.broadcast_to(jnp.sum(spread, axis=1, keepdims=True), spread.shape)
    s = [total[k : k + 1, :] for k in range(8)]
    nu = [s[0], s[1], 2.0 * s[2] - s[0], 2.0 * s[3] - s[1], 2.0 * s[4] - s[0], 2.0 * s[5] - s[1], 2.0 * s[6] - s[0]]
    nu.append(4.0 * s[7] - 2.0 * s[5] - s[1])
    shift = 2.0 * CENTRE / RADIUS
    u = [shift * nu[k] + nu[k + 1] + nu[abs(k - 1)] for k in range(7)]
    mat = [[u[i + j] + u[abs(i - j)] for j in range(BASIS)] for i in range(BASIS)]
    diag = [mat[i][i] for i in range(BASIS)]
    rhs = [(4.0 / RADIUS) * nu[i] for i in range(BASIS)]
    inverse = []
    for k in range(BASIS):
        good = mat[k][k] > 1e-8 * diag[k]
        inv = jnp.where(good, 1.0 / jnp.where(good, mat[k][k], 1.0), 0.0)
        inverse.append(inv)
        for i in range(k + 1, BASIS):
            factor = mat[k][i] * inv
            for j in range(i, BASIS):
                mat[i][j] = mat[i][j] - factor * mat[k][j]
            rhs[i] = rhs[i] - factor * rhs[k]
    out = [None] * BASIS
    for i in reversed(range(BASIS)):
        value = rhs[i]
        for j in range(i + 1, BASIS):
            value = value - mat[i][j] * out[j]
        out[i] = value * inverse[i]
    return out


def kernel(
    n_sec,
    n_slab,
    part_hbm,
    line_hbm,
    flag_hbm,
    instant_ref,
    heat_ref,
    factor_ref,
    dual_ref,
    both_ref,
    part_ref,
    line_ref,
    flag_ref,
    heat,
    coef,
    dual,
    a1,
    a2,
    a3,
    keep,
    mu_a,
    mu_b,
    w_a,
    w_b,
    pick,
    pick_t,
    offered,
    slots,
    back,
    returned,
    sums_ref,
    packed_ref,
    gather,
    local_sem,
    halo_send,
    halo_recv,
    row_send,
    row_recv,
    side_send,
    side_recv,
    sum_send,
    sum_recv,
    ready,
):
    ingots, contact = part_hbm.shape
    melts = n_sec - ingots
    early = 2 * melts // 3
    depth, height, width = heat_ref.shape
    first, last = depth, 2 * depth
    sec, slab = lax.axis_index("sec"), lax.axis_index("slab")
    is_melt = sec < melts
    is_early = sec < early
    has_left, has_right = slab > 0, slab < n_slab - 1
    state_ref, adjoint_ref = both_ref.at[0], both_ref.at[1]

    loads = [
        pltpu.make_async_copy(src, dst.at[pl.ds(first, depth)], local_sem.at[i])
        for i, (src, dst) in enumerate(((heat_ref, heat), (factor_ref, coef), (dual_ref, dual)))
    ]
    tables = [
        pltpu.make_async_copy(src, dst, local_sem.at[3 + i])
        for i, (src, dst) in enumerate(((part_hbm, part_ref), (line_hbm, line_ref), (flag_hbm, flag_ref)))
    ]
    for load in tables + loads:
        load.start()

    barrier = pltpu.get_barrier_semaphore()

    def greet(to_sec, to_slab, sem=barrier):
        pl.semaphore_signal(sem, inc=1, device_id=(to_sec, to_slab), device_id_type=MESH)

    def peer(offset):
        return lax.rem(slab + offset, n_slab)

    @pl.when(is_melt)
    def _():
        pl.when(has_left)(lambda: greet(sec, slab - 1))
        pl.when(has_right)(lambda: greet(sec, slab + 1))

        @pl.when(is_early)
        def _():
            for j in range(ingots):
                greet(melts + j, slab)

    @pl.when(jnp.logical_not(is_melt))
    def _():
        for offset in range(1, n_slab):
            greet(sec, peer(offset))
        for m in range(early, melts):
            greet(m, slab)

    beside = has_left.astype(jnp.int32) + has_right.astype(jnp.int32)
    heard = jnp.where(is_melt, beside + jnp.where(is_early, 0, ingots), n_slab - 1 + early)
    pl.semaphore_wait(barrier, heard)

    def halo(index, src, dst, to_left, to_right):
        (left_src, left_dst), (right_src, right_dst) = to_left, to_right
        send, recv = halo_send.at[index], halo_recv.at[index]
        return (
            pltpu.make_async_remote_copy(
                src_ref=src.at[left_src], dst_ref=dst.at[left_dst], send_sem=send.at[0], recv_sem=recv.at[1],
                device_id=(sec, slab - 1), device_id_type=MESH,
            ),
            pltpu.make_async_remote_copy(
                src_ref=src.at[right_src], dst_ref=dst.at[right_dst], send_sem=send.at[1], recv_sem=recv.at[0],
                device_id=(sec, slab + 1), device_id_type=MESH,
            ),
        )

    def start(pair):
        pl.when(has_left)(lambda: pair[0].start())
        pl.when(has_right)(lambda: pair[1].start())

    def wait_recv(pair):
        pl.when(has_right)(lambda: pair[0].wait_recv())
        pl.when(has_left)(lambda: pair[1].wait_recv())

    def wait_send(pair):
        pl.when(has_left)(lambda: pair[0].wait_send())
        pl.when(has_right)(lambda: pair[1].wait_send())

    def lower(planes, offset=0):
        return pl.ds(offset, planes), pl.ds(last + offset, planes)

    def upper(planes, offset=0):
        at = depth - planes - offset
        return pl.ds(at, planes), pl.ds(at, planes)

    def pass_on(buf, rows, index):
        here = buf.at[pl.ds(first, depth), rows]
        pair = []
        for side, there, to in ((0, last, slab - 1), (1, 0, slab + 1)):
            pair.append(
                pltpu.make_async_remote_copy(
                    src_ref=here, dst_ref=buf.at[pl.ds(there, depth), rows], send_sem=side_send.at[side, index],
                    recv_sem=side_recv.at[1 - side], device_id=(sec, to), device_id_type=MESH,
                )
            )
        start(pair)
        return pair

    def take(buf, side):
        region = buf.at[pl.ds(2 * depth * side, depth)]
        pltpu.make_async_copy(region, region, side_recv.at[side]).wait()

    zero = jnp.zeros((height, width), jnp.float32)

    def clear(*bufs):
        @pl.when(jnp.logical_not(has_left))
        def _():
            for buf in bufs:
                buf[first - 1] = zero

        @pl.when(jnp.logical_not(has_right))
        def _():
            for buf in bufs:
                buf[last] = zero

    row_i = lax.broadcasted_iota(jnp.int32, (contact, contact), 0)
    lane_i = lax.broadcasted_iota(jnp.int32, (contact, contact), 1)

    def column(row):
        return jnp.sum(jnp.where(row_i == lane_i, row, 0.0), axis=1, keepdims=True)

    def slot_rows(index):
        return pl.ds(index * PAIRCAP, PAIRCAP)

    @pl.when(is_melt)
    def _():
        heat_halo = halo(0, heat_ref, heat, lower(depth), upper(depth))
        coef_halo = halo(1, factor_ref, coef, lower(depth - 1), upper(depth - 1))
        edge_halo = halo(2, factor_ref, coef, lower(1, depth - 1), upper(1, depth - 1))
        dual_halo = halo(3, dual_ref, dual, lower(depth), upper(depth))
        start(heat_halo)
        start(coef_halo)

        @pl.when(jnp.logical_not(is_early))
        def _():
            for j in range(ingots):
                greet(melts + j, slab, ready)

        clear(heat, dual, w_a)
        for load in tables:
            load.wait()

        for j in range(ingots):
            named = part_ref[j : j + 1, :].astype(jnp.float32) == sec.astype(jnp.float32)
            lines = line_ref[j : j + 1, :].astype(jnp.float32)
            before = column(jnp.where(named, 1.0, 0.0))
            rank = jnp.sum(jnp.where(row_i < lane_i, before, 0.0), axis=0, keepdims=True)
            slot = lax.broadcasted_iota(jnp.int32, (PAIRCAP, contact), 0).astype(jnp.float32)
            chosen = jnp.where(named, 1.0, 0.0) * jnp.where(rank == slot, 1.0, 0.0)
            slot_line = jnp.sum(chosen * lines, axis=1, keepdims=True)
            live = jnp.sum(chosen, axis=1, keepdims=True)
            q = lax.broadcasted_iota(jnp.int32, (PAIRCAP, height), 1).astype(jnp.float32)
            pick[slot_rows(j), :] = jnp.where(q == slot_line, live, 0.0)
        eye = jnp.where(
            lax.broadcasted_iota(jnp.int32, (height, height), 0) == lax.broadcasted_iota(jnp.int32, (height, height), 1),
            1.0, 0.0,
        )
        pick_t[...] = lax.dot_general(
            eye, pick[...], (((1,), (1,)), ((), ())), precision=HIGHEST, preferred_element_type=jnp.float32
        )

        archived = instant_ref[0].astype(jnp.float32)
        speeds = []
        for k in range(STEPS):
            phase = jnp.full((1, width), archived + k)
            speeds.append(1.0 + 0.5 * jnp.sin(2.0 * math.pi * phase / period_steps))

        for load in loads:
            load.wait()
        wait_recv(heat_halo)
        wait_recv(coef_halo)
        start(edge_halo)
        start(dual_halo)

        states = (heat, a1, a2, a3, state_ref)
        for k in range(STEPS):
            src, dst = states[k], states[k + 1]
            final = k == STEPS - 1
            shift = first if final else 0

            def forward(z, carry, k=k, src=src, dst=dst, shift=shift):
                c = src[z]
                below = src[z - 1]
                total = (below + src[z + 1]) + in_plane(c)
                change = coef[z] * (total - 6.0 * c) - speeds[k] * (c - below)
                bent = jnp.tanh(c)
                dst[z - shift] = c + time_step * change - time_step * sink_rate * bent
                keep[k, z] = 1.0 - time_step * sink_rate * (1.0 - bent * bent)
                return carry

            lax.fori_loop(1 + k, 3 * depth - 1 - k, forward, 0, unroll=2)
            if not final:
                clear(dst)

        for z in range(depth):
            offered[z] = jnp.dot(pick[...], state_ref[z], precision=HIGHEST, preferred_element_type=jnp.float32)
        pl.when(is_early)(lambda: pl.semaphore_wait(ready, ingots))
        sends = []
        for j in range(ingots):
            send = pltpu.make_async_remote_copy(
                src_ref=offered.at[:, slot_rows(j), :],
                dst_ref=slots.at[pl.ds(first, depth), pl.ds(pl.multiple_of(sec * PAIRCAP, PAIRCAP), PAIRCAP), :],
                send_sem=row_send.at[j], recv_sem=row_recv.at[sec], device_id=(melts + j, slab), device_id_type=MESH,
            )
            send.start()
            sends.append(send)
        keep3 = keep.at[3]
        keep_halo = halo(
            4, keep3, keep3, (pl.ds(first, depth - 1), pl.ds(last, depth - 1)), (pl.ds(first + 1, depth - 1), pl.ds(1, depth - 1))
        )
        start(keep_halo)

        for z in (first - 2, last + 1):
            bent = jnp.tanh(a2[z])
            keep[2, z] = 1.0 - time_step * sink_rate * (1.0 - bent * bent)
        wait_recv(edge_halo)
        wait_recv(dual_halo)
        wait_recv(keep_halo)

        passed = []
        for j in reversed(range(ingots)):
            region = returned.at[pl.ds(first, depth), slot_rows(j)]
            pltpu.make_async_copy(region, region, row_recv.at[j]).wait()
            passed.append(pass_on(returned, slot_rows(j), j))

        def add_returned(at):
            for z in range(at, at + depth):
                rows = jnp.dot(pick_t[...], returned[z], precision=HIGHEST, preferred_element_type=jnp.float32)
                value = dual[z] + rows
                dual[z] = value
                w_a[z] = coef[z] * value

        add_returned(first)

        @pl.when(has_left)
        def _():
            take(returned, 0)
            add_returned(0)

        @pl.when(has_right)
        def _():
            take(returned, 1)
            add_returned(last)

        mus = (adjoint_ref, mu_b, mu_a, mu_b, dual)
        ws = (None, w_b, w_a, w_b, w_a)
        for k in reversed(range(STEPS)):
            src, dst, wsrc, wdst = mus[k + 1], mus[k], ws[k + 1], ws[k]
            shift = first if k == 0 else 0

            def backward(z, carry, k=k, src=src, dst=dst, wsrc=wsrc, wdst=wdst, shift=shift):
                c, w = src[z], wsrc[z]
                total = (wsrc[z - 1] + wsrc[z + 1]) + in_plane(w)
                change = total - 6.0 * w - speeds[k] * (c - src[z + 1])
                value = keep[k, z] * c + time_step * change
                dst[z - shift] = value
                if wdst is not None:
                    wdst[z] = coef[z] * value
                return carry

            lax.fori_loop(first - k, last + k, backward, 0, unroll=2)
            if wdst is not None:
                clear(dst, wdst)

        for pair in [heat_halo, coef_halo, edge_halo, dual_halo, keep_halo] + passed:
            wait_send(pair)
        for send in sends:
            send.wait_send()

    @pl.when(jnp.logical_not(is_melt))
    def _():
        dual_halo = halo(3, dual_ref, dual, lower(depth), upper(depth - 1))
        coef_halo = halo(1, factor_ref, coef, lower(depth - 1), upper(depth - 2))
        heat_halo = halo(0, heat_ref, heat, lower(depth), upper(depth - 1))
        start(dual_halo)
        start(coef_halo)
        for m in range(early):
            greet(m, slab, ready)
        clear(heat, dual)

        for load in tables:
            load.wait()
        mine = sec - melts
        names = part_ref[pl.ds(mine, 1), :].astype(jnp.float32)
        flags = flag_ref[pl.ds(mine, 1), :].astype(jnp.float32)
        names_col, flags_col = column(names), column(flags)
        same = jnp.where(names_col == names, 1.0, 0.0)
        rank_col = jnp.sum(jnp.where(lane_i < row_i, same, 0.0), axis=1, keepdims=True)
        rank_row = jnp.sum(jnp.where(row_i < lane_i, same, 0.0), axis=0, keepdims=True)
        count = melts * PAIRCAP
        slot_lane = lax.broadcasted_iota(jnp.int32, (contact, count), 1).astype(jnp.float32)
        slot_row = lax.broadcasted_iota(jnp.int32, (count, contact), 0).astype(jnp.float32)
        place = jnp.where(slot_lane == names_col * PAIRCAP + rank_col, flags_col, 0.0)
        give = jnp.where(slot_row == names * PAIRCAP + rank_row, flags, 0.0)

        for load in loads:
            load.wait()
        wait_recv(dual_halo)
        wait_recv(coef_halo)
        start(heat_halo)

        def solve(which, t0, out):
            ts = (t0, a1, a2, a3)

            def image(t, z):
                c = t[z]
                return (coef[z] - (CENTRE - 6.0)) * c - ((t[z - 1] + t[z + 1]) + in_plane(c))

            for k in range(1, BASIS):

                def grow(z, carry, k=k):
                    value = image(ts[k - 1], z)
                    if k == 1:
                        ts[k][z] = value * (1.0 / RADIUS)
                    else:
                        ts[k][z] = value * (2.0 / RADIUS) - ts[k - 2][z]
                    return carry

                reach = BASIS - 1 - k
                lax.fori_loop(first - reach, last + 1 + reach, grow, 0, unroll=2)
                clear(ts[k])

            def dots(z, sums):
                t = [ref[z] for ref in ts]
                image3 = (coef[z] - (CENTRE - 6.0)) * t[3] - 2.0 * a3[z + 1] - in_plane(t[3])
                terms = (
                    t[0] * t[0], t[0] * t[1], t[1] * t[1], t[1] * t[2],
                    t[2] * t[2], t[2] * t[3], t[3] * t[3], t[3] * image3 * (1.0 / RADIUS),
                )
                return tuple(s + fold(term) for s, term in zip(sums, terms))

            sums = lax.fori_loop(first, last, dots, (jnp.zeros((8, width), jnp.float32),) * 8, unroll=2)
            for k in range(8):
                sums_ref[pl.ds(k, 1), :] = jnp.sum(sums[k], axis=0, keepdims=True)
            packed = pack(sums_ref[...])
            packed_ref[which] = packed
            for offset in range(1, n_slab):
                pltpu.make_async_remote_copy(
                    src_ref=packed_ref.at[which], dst_ref=gather.at[which, pl.ds(offset - 1, 1)],
                    send_sem=sum_send.at[which], recv_sem=sum_recv.at[which],
                    device_id=(sec, peer(offset)), device_id_type=MESH,
                ).start()
            others = gather.at[which, pl.ds(0, n_slab - 1)]
            pltpu.make_async_copy(others, others, sum_recv.at[which]).wait()
            c = coefficients(packed + jnp.sum(gather[which, : n_slab - 1, :], axis=0, keepdims=True))

            def combine(z, carry):
                out[z - first] = (c[0] * ts[0][z] + c[1] * ts[1][z]) + (c[2] * ts[2][z] + c[3] * ts[3][z])
                return carry

            lax.fori_loop(first, last, combine, 0, unroll=2)

        solve(0, dual, adjoint_ref)
        for z in range(depth):
            back[z] = jnp.dot(give, adjoint_ref[z, :contact, :], precision=HIGHEST, preferred_element_type=jnp.float32)
        sends = []
        for m in range(melts):
            if m == early:
                pl.semaphore_wait(ready, melts - early)
            send = pltpu.make_async_remote_copy(
                src_ref=back.at[:, slot_rows(m), :],
                dst_ref=returned.at[pl.ds(first, depth), pl.ds(pl.multiple_of(mine * PAIRCAP, PAIRCAP), PAIRCAP), :],
                send_sem=row_send.at[m], recv_sem=row_recv.at[mine], device_id=(m, slab), device_id_type=MESH,
            )
            send.start()
            sends.append(send)

        passed = []
        for m in range(melts):
            region = slots.at[pl.ds(first, depth), slot_rows(m)]
            pltpu.make_async_copy(region, region, row_recv.at[m]).wait()
            passed.append(pass_on(slots, slot_rows(m), m))

        def load_up(at):
            for z in range(at, at + depth):
                rows = jnp.dot(place, slots[z], precision=HIGHEST, preferred_element_type=jnp.float32)
                heat[z, pl.ds(0, contact), :] = heat[z, pl.ds(0, contact), :] + rows

        wait_recv(heat_halo)
        load_up(first)

        @pl.when(has_left)
        def _():
            take(slots, 0)
            load_up(0)

        @pl.when(has_right)
        def _():
            take(slots, 1)
            load_up(last)

        solve(1, heat, state_ref)

        for pair in [dual_halo, coef_halo, heat_halo] + passed:
            wait_send(pair)
        for send in sends:
            send.wait_send()
        for which in range(2):
            others = gather.at[which, pl.ds(0, n_slab - 1)]
            pltpu.make_async_copy(others, others, sum_send.at[which]).wait()


def body(n_sec, n_slab, heat_level, material_factor, dual_sensitivity, part, line, flag, instant):
    ingots, contact = line.shape
    melts = n_sec - ingots
    _, depth, height, width = heat_level.shape
    f32 = jnp.float32
    wide = pltpu.VMEM((3 * depth, height, width), f32)
    table = pltpu.VMEM((ingots, contact), jnp.int32)
    dma = pltpu.SemaphoreType.DMA
    most = max(melts, ingots)
    scratch = [
        table, table, table,
        wide, wide, wide, wide, wide, wide,
        pltpu.VMEM((STEPS, 3 * depth, height, width), f32),
        wide, wide, wide, wide,
        pltpu.VMEM((ingots * PAIRCAP, height), f32),
        pltpu.VMEM((height, ingots * PAIRCAP), f32),
        pltpu.VMEM((depth, ingots * PAIRCAP, width), f32),
        pltpu.VMEM((3 * depth, melts * PAIRCAP, width), f32),
        pltpu.VMEM((depth, melts * PAIRCAP, width), f32),
        pltpu.VMEM((3 * depth, ingots * PAIRCAP, width), f32),
        pltpu.VMEM((8, width), f32),
        pltpu.VMEM((2, 1, width), f32),
        pltpu.VMEM((2, n_slab, width), f32),
        dma((6,)), dma((5, 2)), dma((5, 2)),
        dma((most,)), dma((most,)), dma((2, most)), dma((2,)),
        dma((2,)), dma((2,)), pltpu.SemaphoreType.REGULAR,
    ]
    hbm, vmem, smem = (pl.BlockSpec(memory_space=s) for s in (pltpu.HBM, pltpu.VMEM, pltpu.SMEM))
    fields = (part[:, :, 0], line, flag, heat_level[0], material_factor[0], dual_sensitivity[0])
    fields = [pltpu.with_memory_space_constraint(field, pltpu.HBM) for field in fields]
    both = pl.pallas_call(
        functools.partial(kernel, n_sec, n_slab),
        out_shape=jax.ShapeDtypeStruct((2, depth, height, width), f32),
        in_specs=[hbm, hbm, hbm, smem, hbm, hbm, hbm],
        out_specs=vmem,
        scratch_shapes=scratch,
        compiler_params=pltpu.CompilerParams(
            collective_id=0, has_side_effects=True, vmem_limit_bytes=32 * 1024 * 1024
        ),
    )(*fields[:3], instant, *fields[3:])
    return both[0:1], both[1:2]


def solution(mesh):
    n_sec, n_slab = mesh.shape["sec"], mesh.shape["slab"]
    fields = P("sec", "slab", None, None)
    return jax.shard_map(
        functools.partial(body, n_sec, n_slab),
        mesh=mesh,
        in_specs=(fields, fields, fields, P(), P(), P(), P()),
        out_specs=(fields, fields),
        check_vma=False,
    )
```

time: 52.4 us -> 43.5 us (0.83)
  Pallas kernels: 48.7 us -> 41.2 us
  local copies, waits for them, and re-layouts: 2.26 us -> 0.72 us
    pallas_call x1, Pallas kernels: 48.7 us -> 41.2 us  [body(): pl.pallas_call(functools.partial(kernel, n_sec, n_slab), out_shape=jax.Sh...]
    unnamed x4 -> x0, local copies, waits for them, and re-layouts: 2.26 us -> none
    slice x0 -> x1, local copies, waits for them, and re-layouts: none -> 0.72 us  [body(): return (both[0:1], both[1:2])]
where the time goes in v3:
time: 43.5 us; the launch traced here: 43.3 us
  Pallas kernels  41.2 us (95%)
  between operations  1.29 us (3%)
  local copies, waits for them, and re-layouts  0.72 us (2%)
    pallas_call x1, Pallas kernels, body(): pl.pallas_call(functools.partial(kernel, n_sec, n_slab), out_shape=jax.Sh...  41.2 us

profile of v3, /device:TPU:1, one launch (start us, length us, event | category | flops | bytes accessed | tf_op | source)
XLA Modules:
  0.0 43.3 jit_solution(14184597580430298346)
XLA Ops:
  1.3 41.2 %shard_map.86 = f32[2,4,64,128]{3,2,1,0:T(8,128)S(1)} custom-call(s32[4,48]{1,0:T(4,128)} %bitcast.7, s32[4,48]{1,0:T(4,128)} %line_hbm.1, s32[4,48]{1,0:T(4,128)} %flag_hbm.1, s32[1]{0:T(128)S(6)} %copy.9.instant_ref, f32[4,64,128]{2,1,0:T(8,128)} %bitcast.4, f32[4,64,128]{2,1,0:T(8,128)} %bitcast.5, f32[4,64,128]{2,1,0:T(8,128)} %bitcast.6), custom_call_target="tpu_custom_call" | custom-call | tf_op jit(solution)/shard_map/pallas_call | solution.py:562
  42.5 0.7 %fusion = (f32[1,4,64,128]{3,2,1,0:T(8,128)}, f32[1,4,64,128]{3,2,1,0:T(8,128)}) fusion(f32[2,4,64,128]{3,2,1,0:T(8,128)S(1)} %shard_map.86), kind=kLoop, calls=%fused_computation | loop fusion | bytes 524288 | tf_op jit(solution)/shard_map/slice | solution.py:572

commit v4 on v3

--- a/solution.py
+++ b/solution.py
@@ -11,6 +11,7 @@
 STEPS = 4
 PAIRCAP = 8
 BASIS = 4
+CLOSE = 4
 
 time_step = 0.1
 sink_rate = 0.5
@@ -113,6 +114,7 @@
     offered,
     slots,
     back,
+    basis_rows,
     returned,
     sums_ref,
     packed_ref,
@@ -127,6 +129,7 @@
     sum_send,
     sum_recv,
     ready,
+    known,
 ):
     ingots, contact = part_hbm.shape
     melts = n_sec - ingots
@@ -147,16 +150,32 @@
         pltpu.make_async_copy(src, dst, local_sem.at[3 + i])
         for i, (src, dst) in enumerate(((part_hbm, part_ref), (line_hbm, line_ref), (flag_hbm, flag_ref)))
     ]
-    for load in tables + loads:
-        load.start()
-
     barrier = pltpu.get_barrier_semaphore()
 
     def greet(to_sec, to_slab, sem=barrier):
         pl.semaphore_signal(sem, inc=1, device_id=(to_sec, to_slab), device_id_type=MESH)
 
-    def peer(offset):
-        return lax.rem(slab + offset, n_slab)
+    def along(offset):
+        return lax.rem(slab + offset % n_slab, n_slab)
+
+    sizes = (4, 4, 2) if n_slab == 32 else (n_slab,)
+    partners = []
+    for flat in range(1, n_slab):
+        shift, rest = [], flat
+        for size in reversed(sizes):
+            shift.insert(0, rest % size)
+            rest //= size
+        partners.append((sum(min(step, size - step) for step, size in zip(shift, sizes)), tuple(shift)))
+    partners.sort(key=lambda entry: (-entry[0], entry[1]))
+
+    def partner(shift):
+        index, stride, rest = 0, 1, slab
+        for step, size in zip(reversed(shift), reversed(sizes)):
+            index = index + lax.rem(lax.rem(rest, size) + step, size) * stride
+            rest, stride = rest // size, stride * size
+        return index
+
+    near = sorted({offset % n_slab for offset in range(-CLOSE, CLOSE + 1)} - {0})
 
     @pl.when(is_melt)
     def _():
@@ -170,13 +189,15 @@
 
     @pl.when(jnp.logical_not(is_melt))
     def _():
-        for offset in range(1, n_slab):
-            greet(sec, peer(offset))
+        for offset in near:
+            greet(sec, along(offset))
         for m in range(early, melts):
             greet(m, slab)
 
     beside = has_left.astype(jnp.int32) + has_right.astype(jnp.int32)
-    heard = jnp.where(is_melt, beside + jnp.where(is_early, 0, ingots), n_slab - 1 + early)
+    heard = jnp.where(is_melt, beside + jnp.where(is_early, 0, ingots), len(near) + early)
+    for load in tables + loads:
+        load.start()
     pl.semaphore_wait(barrier, heard)
 
     def halo(index, src, dst, to_left, to_right):
@@ -398,13 +419,29 @@
 
     @pl.when(jnp.logical_not(is_melt))
     def _():
-        dual_halo = halo(3, dual_ref, dual, lower(depth), upper(depth - 1))
-        coef_halo = halo(1, factor_ref, coef, lower(depth - 1), upper(depth - 2))
+        dual_near = halo(3, dual_ref, dual, lower(2), upper(2))
+        coef_near = halo(1, factor_ref, coef, lower(1), upper(1))
+        dual_far = halo(4, dual_ref, dual, lower(depth - 2, 2), upper(depth - 3, 2))
+        coef_far = halo(2, factor_ref, coef, lower(depth - 2, 1), upper(depth - 3, 1))
         heat_halo = halo(0, heat_ref, heat, lower(depth), upper(depth - 1))
-        start(dual_halo)
-        start(coef_halo)
+        start(dual_near)
+        start(coef_near)
+        start(coef_far)
+        start(dual_far)
         for m in range(early):
             greet(m, slab, ready)
+        rounds = []
+        reach = CLOSE
+        while reach < n_slab // 2:
+            rounds.append(reach)
+            reach *= 2
+
+        def tell(index):
+            for offset in (-rounds[index], rounds[index]):
+                greet(sec, along(offset), known.at[index])
+
+        if rounds:
+            tell(0)
         clear(heat, dual)
 
         for load in tables:
@@ -424,54 +461,72 @@
 
         for load in loads:
             load.wait()
-        wait_recv(dual_halo)
-        wait_recv(coef_halo)
-        start(heat_halo)
-
-        def solve(which, t0, out):
+        for index in range(len(rounds)):
+            pl.semaphore_wait(known.at[index], 2)
+            if index + 1 < len(rounds):
+                tell(index + 1)
+
+        def solve(which, t0, out, arrive_near, arrive_far, meanwhile, then):
             ts = (t0, a1, a2, a3)
 
-            def image(t, z):
+            def grow(k, z):
+                t = ts[k - 1]
                 c = t[z]
-                return (coef[z] - (CENTRE - 6.0)) * c - ((t[z - 1] + t[z + 1]) + in_plane(c))
-
-            for k in range(1, BASIS):
-
-                def grow(z, carry, k=k):
-                    value = image(ts[k - 1], z)
-                    if k == 1:
-                        ts[k][z] = value * (1.0 / RADIUS)
-                    else:
-                        ts[k][z] = value * (2.0 / RADIUS) - ts[k - 2][z]
-                    return carry
-
-                reach = BASIS - 1 - k
-                lax.fori_loop(first - reach, last + 1 + reach, grow, 0, unroll=2)
-                clear(ts[k])
-
-            def dots(z, sums):
-                t = [ref[z] for ref in ts]
-                image3 = (coef[z] - (CENTRE - 6.0)) * t[3] - 2.0 * a3[z + 1] - in_plane(t[3])
-                terms = (
-                    t[0] * t[0], t[0] * t[1], t[1] * t[1], t[1] * t[2],
-                    t[2] * t[2], t[2] * t[3], t[3] * t[3], t[3] * image3 * (1.0 / RADIUS),
-                )
-                return tuple(s + fold(term) for s, term in zip(sums, terms))
-
-            sums = lax.fori_loop(first, last, dots, (jnp.zeros((8, width), jnp.float32),) * 8, unroll=2)
+                value = (coef[z] - (CENTRE - 6.0)) * c - ((t[z - 1] + t[z + 1]) + in_plane(c))
+                if k == 1:
+                    ts[k][z] = value * (1.0 / RADIUS)
+                else:
+                    ts[k][z] = value * (2.0 / RADIUS) - ts[k - 2][z]
+
+            def grow_all(k, lo, hi):
+                lax.fori_loop(lo, hi, lambda z, carry: grow(k, z) or carry, 0, unroll=2)
+
+            def add_up(terms, count):
+                def plane(z, sums):
+                    return tuple(s + fold(term) for s, term in zip(sums, terms(z)))
+
+                sums = lax.fori_loop(first, last, plane, (jnp.zeros((8, width), jnp.float32),) * count, unroll=2)
+                return [jnp.sum(total, axis=0, keepdims=True) for total in sums]
+
+            def near_terms(z):
+                x0, x1, x2 = (ref[z] for ref in ts[:3])
+                return x0 * x0, x0 * x1, x1 * x1, x1 * x2, x2 * x2
+
+            def far_terms(z):
+                x2, x3 = a2[z], a3[z]
+                image = (coef[z] - (CENTRE - 6.0)) * x3 - 2.0 * a3[z + 1] - in_plane(x3)
+                return x2 * x3, x3 * x3, x3 * image * (1.0 / RADIUS)
+
+            arrive_near()
+            grow_all(1, first - 1, last + 1)
+            clear(a1)
+            grow_all(2, first, last)
+            sums = add_up(near_terms, 5)
+            arrive_far()
+            for z in (first - 2, last + 1, last + 2):
+                grow(1, z)
+            for z in (first - 1, last, last + 1):
+                grow(2, z)
+            clear(a2)
+            grow_all(3, first, last)
+            grow(3, last)
+            clear(a3)
+            sums += add_up(far_terms, 3)
             for k in range(8):
-                sums_ref[pl.ds(k, 1), :] = jnp.sum(sums[k], axis=0, keepdims=True)
+                sums_ref[pl.ds(k, 1), :] = sums[k]
             packed = pack(sums_ref[...])
             packed_ref[which] = packed
-            for offset in range(1, n_slab):
+            for index, (_, shift) in enumerate(partners):
                 pltpu.make_async_remote_copy(
-                    src_ref=packed_ref.at[which], dst_ref=gather.at[which, pl.ds(offset - 1, 1)],
+                    src_ref=packed_ref.at[which], dst_ref=gather.at[which, pl.ds(index, 1)],
                     send_sem=sum_send.at[which], recv_sem=sum_recv.at[which],
-                    device_id=(sec, peer(offset)), device_id_type=MESH,
+                    device_id=(sec, partner(shift)), device_id_type=MESH,
                 ).start()
+            meanwhile()
             others = gather.at[which, pl.ds(0, n_slab - 1)]
             pltpu.make_async_copy(others, others, sum_recv.at[which]).wait()
             c = coefficients(packed + jnp.sum(gather[which, : n_slab - 1, :], axis=0, keepdims=True))
+            then(c)
 
             def combine(z, carry):
                 out[z - first] = (c[0] * ts[0][z] + c[1] * ts[1][z]) + (c[2] * ts[2][z] + c[3] * ts[3][z])
@@ -479,20 +534,41 @@
 
             lax.fori_loop(first, last, combine, 0, unroll=2)
 
-        solve(0, dual, adjoint_ref)
-        for z in range(depth):
-            back[z] = jnp.dot(give, adjoint_ref[z, :contact, :], precision=HIGHEST, preferred_element_type=jnp.float32)
+        def arrive_near():
+            wait_recv(dual_near)
+            wait_recv(coef_near)
+
+        def arrive_far():
+            wait_recv(coef_far)
+            wait_recv(dual_far)
+            start(heat_halo)
+
+        def pick_basis():
+            for i, t in enumerate((dual, a1, a2, a3)):
+                for z in range(depth):
+                    basis_rows[i, z] = jnp.dot(
+                        give, t[first + z, :contact, :], precision=HIGHEST, preferred_element_type=jnp.float32
+                    )
+
         sends = []
-        for m in range(melts):
-            if m == early:
-                pl.semaphore_wait(ready, melts - early)
-            send = pltpu.make_async_remote_copy(
-                src_ref=back.at[:, slot_rows(m), :],
-                dst_ref=returned.at[pl.ds(first, depth), pl.ds(pl.multiple_of(mine * PAIRCAP, PAIRCAP), PAIRCAP), :],
-                send_sem=row_send.at[m], recv_sem=row_recv.at[mine], device_id=(m, slab), device_id_type=MESH,
-            )
-            send.start()
-            sends.append(send)
+
+        def send_back(c):
+            for z in range(depth):
+                back[z] = (c[0] * basis_rows[0, z] + c[1] * basis_rows[1, z]) + (
+                    c[2] * basis_rows[2, z] + c[3] * basis_rows[3, z]
+                )
+            for m in range(melts):
+                if m == early:
+                    pl.semaphore_wait(ready, melts - early)
+                send = pltpu.make_async_remote_copy(
+                    src_ref=back.at[:, slot_rows(m), :],
+                    dst_ref=returned.at[pl.ds(first, depth), pl.ds(pl.multiple_of(mine * PAIRCAP, PAIRCAP), PAIRCAP), :],
+                    send_sem=row_send.at[m], recv_sem=row_recv.at[mine], device_id=(m, slab), device_id_type=MESH,
+                )
+                send.start()
+                sends.append(send)
+
+        solve(0, dual, adjoint_ref, arrive_near, arrive_far, pick_basis, send_back)
 
         passed = []
         for m in range(melts):
@@ -518,9 +594,9 @@
             take(slots, 1)
             load_up(last)
 
-        solve(1, heat, state_ref)
-
-        for pair in [dual_halo, coef_halo, heat_halo] + passed:
+        solve(1, heat, state_ref, lambda: None, lambda: None, lambda: None, lambda c: None)
+
+        for pair in [dual_near, coef_near, dual_far, coef_far, heat_halo] + passed:
             wait_send(pair)
         for send in sends:
             send.wait_send()
@@ -548,13 +624,14 @@
         pltpu.VMEM((depth, ingots * PAIRCAP, width), f32),
         pltpu.VMEM((3 * depth, melts * PAIRCAP, width), f32),
         pltpu.VMEM((depth, melts * PAIRCAP, width), f32),
+        pltpu.VMEM((BASIS, depth, melts * PAIRCAP, width), f32),
         pltpu.VMEM((3 * depth, ingots * PAIRCAP, width), f32),
         pltpu.VMEM((8, width), f32),
         pltpu.VMEM((2, 1, width), f32),
         pltpu.VMEM((2, n_slab, width), f32),
         dma((6,)), dma((5, 2)), dma((5, 2)),
         dma((most,)), dma((most,)), dma((2, most)), dma((2,)),
-        dma((2,)), dma((2,)), pltpu.SemaphoreType.REGULAR,
+        dma((2,)), dma((2,)), pltpu.SemaphoreType.REGULAR, pltpu.SemaphoreType.REGULAR((4,)),
     ]
     hbm, vmem, smem = (pl.BlockSpec(memory_space=s) for s in (pltpu.HBM, pltpu.VMEM, pltpu.SMEM))
     fields = (part[:, :, 0], line, flag, heat_level[0], material_factor[0], dual_sensitivity[0])

time: 43.5 us -> 43.5 us (level)
  the two profiles are of different devices: /device:TPU:1 before, /device:TPU:104 now
where the time goes in v4:
time: 43.5 us; the launch traced here: 43.3 us
  Pallas kernels  41.3 us (95%)
  between operations  1.29 us (3%)
  local copies, waits for them, and re-layouts  0.72 us (2%)
    pallas_call x1, Pallas kernels, body(): pl.pallas_call(functools.partial(kernel, n_sec, n_slab), out_shape=jax.Sh...  41.3 us

profile of v4, /device:TPU:104, one launch (start us, length us, event | category | flops | bytes accessed | tf_op | source)
XLA Modules:
  0.0 43.3 jit_solution(10497287553466865700)
XLA Ops:
  1.3 41.3 %shard_map.86 = f32[2,4,64,128]{3,2,1,0:T(8,128)S(1)} custom-call(s32[4,48]{1,0:T(4,128)} %bitcast.7, s32[4,48]{1,0:T(4,128)} %line_hbm.1, s32[4,48]{1,0:T(4,128)} %flag_hbm.1, s32[1]{0:T(128)S(6)} %copy.9.instant_ref, f32[4,64,128]{2,1,0:T(8,128)} %bitcast.4, f32[4,64,128]{2,1,0:T(8,128)} %bitcast.5, f32[4,64,128]{2,1,0:T(8,128)} %bitcast.6), custom_call_target="tpu_custom_call" | custom-call | tf_op jit(solution)/shard_map/pallas_call | solution.py:639
  42.6 0.7 %fusion = (f32[1,4,64,128]{3,2,1,0:T(8,128)}, f32[1,4,64,128]{3,2,1,0:T(8,128)}) fusion(f32[2,4,64,128]{3,2,1,0:T(8,128)S(1)} %shard_map.86), kind=kLoop, calls=%fused_computation | loop fusion | bytes 524288 | tf_op jit(solution)/shard_map/slice | solution.py:649

commit v5 on v4

--- a/solution.py
+++ b/solution.py
@@ -84,6 +84,12 @@
     return out
 
 
+def relays(n_sec, ingots):
+    if (n_sec, ingots) != (16, 4):
+        return []
+    return [(3, 5), (2, 5), (3, 6), (1, 5), (2, 6), (0, 4)]
+
+
 def kernel(
     n_sec,
     n_slab,
@@ -105,16 +111,20 @@
     a2,
     a3,
     keep,
-    mu_a,
-    mu_b,
-    w_a,
-    w_b,
+    mu3,
+    mu2,
+    mu1,
+    w4,
+    w3,
+    w2,
+    w1,
     pick,
     pick_t,
     offered,
     slots,
     back,
     basis_rows,
+    relay,
     returned,
     sums_ref,
     packed_ref,
@@ -130,6 +140,8 @@
     sum_recv,
     ready,
     known,
+    relay_send,
+    relay_recv,
 ):
     ingots, contact = part_hbm.shape
     melts = n_sec - ingots
@@ -139,6 +151,8 @@
     sec, slab = lax.axis_index("sec"), lax.axis_index("slab")
     is_melt = sec < melts
     is_early = sec < early
+    relayed = relays(n_sec, ingots)
+    targets = sorted({m for _, m in relayed})
     has_left, has_right = slab > 0, slab < n_slab - 1
     state_ref, adjoint_ref = both_ref.at[0], both_ref.at[1]
 
@@ -187,6 +201,9 @@
             for j in range(ingots):
                 greet(melts + j, slab)
 
+        for m in targets:
+            pl.when(sec == m)(lambda: greet(early, slab))
+
     @pl.when(jnp.logical_not(is_melt))
     def _():
         for offset in near:
@@ -196,6 +213,7 @@
 
     beside = has_left.astype(jnp.int32) + has_right.astype(jnp.int32)
     heard = jnp.where(is_melt, beside + jnp.where(is_early, 0, ingots), len(near) + early)
+    heard = heard + jnp.where(sec == early, len(targets), 0) if targets else heard
     for load in tables + loads:
         load.start()
     pl.semaphore_wait(barrier, heard)
@@ -286,7 +304,7 @@
             for j in range(ingots):
                 greet(melts + j, slab, ready)
 
-        clear(heat, dual, w_a)
+        clear(heat, dual, w4)
         for load in tables:
             load.wait()
 
@@ -367,6 +385,21 @@
         wait_recv(dual_halo)
         wait_recv(keep_halo)
 
+        def relay_on(index):
+            j, m = relayed[index]
+            return pltpu.make_async_remote_copy(
+                src_ref=relay.at[index], dst_ref=returned.at[pl.ds(first, depth), slot_rows(j), :],
+                send_sem=relay_send.at[index], recv_sem=row_recv.at[j], device_id=(m, slab), device_id_type=MESH,
+            )
+
+        if relayed:
+
+            @pl.when(sec == early)
+            def _():
+                for index in range(len(relayed)):
+                    pltpu.make_async_copy(relay.at[index], relay.at[index], relay_recv.at[index]).wait()
+                    relay_on(index).start()
+
         passed = []
         for j in reversed(range(ingots)):
             region = returned.at[pl.ds(first, depth), slot_rows(j)]
@@ -378,27 +411,17 @@
                 rows = jnp.dot(pick_t[...], returned[z], precision=HIGHEST, preferred_element_type=jnp.float32)
                 value = dual[z] + rows
                 dual[z] = value
-                w_a[z] = coef[z] * value
+                w4[z] = coef[z] * value
 
         add_returned(first)
 
-        @pl.when(has_left)
-        def _():
-            take(returned, 0)
-            add_returned(0)
-
-        @pl.when(has_right)
-        def _():
-            take(returned, 1)
-            add_returned(last)
-
-        mus = (adjoint_ref, mu_b, mu_a, mu_b, dual)
-        ws = (None, w_b, w_a, w_b, w_a)
-        for k in reversed(range(STEPS)):
+        mus, ws = (adjoint_ref, mu1, mu2, mu3, dual), (None, w1, w2, w3, w4)
+
+        def backward(k, lo, hi):
             src, dst, wsrc, wdst = mus[k + 1], mus[k], ws[k + 1], ws[k]
             shift = first if k == 0 else 0
 
-            def backward(z, carry, k=k, src=src, dst=dst, wsrc=wsrc, wdst=wdst, shift=shift):
+            def plane(z, carry):
                 c, w = src[z], wsrc[z]
                 total = (wsrc[z - 1] + wsrc[z + 1]) + in_plane(w)
                 change = total - 6.0 * w - speeds[k] * (c - src[z + 1])
@@ -408,9 +431,46 @@
                     wdst[z] = coef[z] * value
                 return carry
 
-            lax.fori_loop(first - k, last + k, backward, 0, unroll=2)
+            lax.fori_loop(lo, hi, plane, 0, unroll=2)
             if wdst is not None:
                 clear(dst, wdst)
+
+        @pl.when(slab % 2 == 0)
+        def _():
+            take(returned, 1)
+            add_returned(last)
+            for k in (3, 2, 1):
+                backward(k, first + STEPS - k, last + k)
+
+            @pl.when(has_left)
+            def _():
+                take(returned, 0)
+                add_returned(0)
+
+            for k in (3, 2, 1, 0):
+                backward(k, first - k, first + STEPS - k)
+
+        @pl.when(slab % 2 == 1)
+        def _():
+            take(returned, 0)
+            add_returned(0)
+            for k in (3, 2, 1):
+                backward(k, first - k, last - STEPS + k)
+
+            @pl.when(has_right)
+            def _():
+                take(returned, 1)
+                add_returned(last)
+
+            for k in (3, 2, 1, 0):
+                backward(k, last - STEPS + k, last + k)
+
+        if relayed:
+
+            @pl.when(sec == early)
+            def _():
+                for index in range(len(relayed)):
+                    relay_on(index).wait_send()
 
         for pair in [heat_halo, coef_halo, edge_halo, dual_halo, keep_halo] + passed:
             wait_send(pair)
@@ -557,15 +617,27 @@
                 back[z] = (c[0] * basis_rows[0, z] + c[1] * basis_rows[1, z]) + (
                     c[2] * basis_rows[2, z] + c[3] * basis_rows[3, z]
                 )
+            pl.semaphore_wait(ready, melts - early)
+            for index, (j, m) in enumerate(relayed):
+
+                @pl.when(mine == j)
+                def _():
+                    pltpu.make_async_remote_copy(
+                        src_ref=back.at[:, slot_rows(m), :], dst_ref=relay.at[index], send_sem=row_send.at[m],
+                        recv_sem=relay_recv.at[index], device_id=(early, slab), device_id_type=MESH,
+                    ).start()
+
             for m in range(melts):
-                if m == early:
-                    pl.semaphore_wait(ready, melts - early)
+                direct = [j for j in range(ingots) if (j, m) not in relayed]
                 send = pltpu.make_async_remote_copy(
                     src_ref=back.at[:, slot_rows(m), :],
                     dst_ref=returned.at[pl.ds(first, depth), pl.ds(pl.multiple_of(mine * PAIRCAP, PAIRCAP), PAIRCAP), :],
                     send_sem=row_send.at[m], recv_sem=row_recv.at[mine], device_id=(m, slab), device_id_type=MESH,
                 )
-                send.start()
+                if len(direct) == ingots:
+                    send.start()
+                elif direct:
+                    pl.when(functools.reduce(jnp.logical_or, [mine == j for j in direct]))(lambda send=send: send.start())
                 sends.append(send)
 
         solve(0, dual, adjoint_ref, arrive_near, arrive_far, pick_basis, send_back)
@@ -618,13 +690,14 @@
         table, table, table,
         wide, wide, wide, wide, wide, wide,
         pltpu.VMEM((STEPS, 3 * depth, height, width), f32),
-        wide, wide, wide, wide,
+        wide, wide, wide, wide, wide, wide, wide,
         pltpu.VMEM((ingots * PAIRCAP, height), f32),
         pltpu.VMEM((height, ingots * PAIRCAP), f32),
         pltpu.VMEM((depth, ingots * PAIRCAP, width), f32),
         pltpu.VMEM((3 * depth, melts * PAIRCAP, width), f32),
         pltpu.VMEM((depth, melts * PAIRCAP, width), f32),
         pltpu.VMEM((BASIS, depth, melts * PAIRCAP, width), f32),
+        pltpu.VMEM((max(len(relays(n_sec, ingots)), 1), depth, PAIRCAP, width), f32),
         pltpu.VMEM((3 * depth, ingots * PAIRCAP, width), f32),
         pltpu.VMEM((8, width), f32),
         pltpu.VMEM((2, 1, width), f32),
@@ -632,6 +705,7 @@
         dma((6,)), dma((5, 2)), dma((5, 2)),
         dma((most,)), dma((most,)), dma((2, most)), dma((2,)),
         dma((2,)), dma((2,)), pltpu.SemaphoreType.REGULAR, pltpu.SemaphoreType.REGULAR((4,)),
+        dma((8,)), dma((8,)),
     ]
     hbm, vmem, smem = (pl.BlockSpec(memory_space=s) for s in (pltpu.HBM, pltpu.VMEM, pltpu.SMEM))
     fields = (part[:, :, 0], line, flag, heat_level[0], material_factor[0], dual_sensitivity[0])

time: 43.5 us -> 44.4 us (1.021)
  the two profiles are of different devices: /device:TPU:104 before, /device:TPU:129 now
where the time goes in v5:
time: 44.4 us; the launch traced here: 44.2 us
  Pallas kernels  42.2 us (95%)
  between operations  1.29 us (3%)
  local copies, waits for them, and re-layouts  0.72 us (2%)
    pallas_call x1, Pallas kernels, body(): pl.pallas_call(functools.partial(kernel, n_sec, n_slab), out_shape=jax.Sh...  42.2 us

profile of v5, /device:TPU:129, one launch (start us, length us, event | category | flops | bytes accessed | tf_op | source)
XLA Modules:
  0.0 44.2 jit_solution(7437245451879640226)
XLA Ops:
  1.3 42.2 %shard_map.86 = f32[2,4,64,128]{3,2,1,0:T(8,128)S(1)} custom-call(s32[4,48]{1,0:T(4,128)} %bitcast.7, s32[4,48]{1,0:T(4,128)} %line_hbm.1, s32[4,48]{1,0:T(4,128)} %flag_hbm.1, s32[1]{0:T(128)S(6)} %copy.9.instant_ref, f32[4,64,128]{2,1,0:T(8,128)} %bitcast.4, f32[4,64,128]{2,1,0:T(8,128)} %bitcast.5, f32[4,64,128]{2,1,0:T(8,128)} %bitcast.6), custom_call_target="tpu_custom_call" | custom-call | tf_op jit(solution)/shard_map/pallas_call | solution.py:713
  43.5 0.7 %fusion = (f32[1,4,64,128]{3,2,1,0:T(8,128)}, f32[1,4,64,128]{3,2,1,0:T(8,128)}) fusion(f32[2,4,64,128]{3,2,1,0:T(8,128)S(1)} %shard_map.86), kind=kLoop, calls=%fused_computation | loop fusion | bytes 524288 | tf_op jit(solution)/shard_map/slice | solution.py:723

commit v6 on v5

--- a/solution.py
+++ b/solution.py
@@ -87,7 +87,7 @@
 def relays(n_sec, ingots):
     if (n_sec, ingots) != (16, 4):
         return []
-    return [(3, 5), (2, 5), (3, 6), (1, 5), (2, 6), (0, 4)]
+    return [(1, 5), (2, 5), (3, 5), (2, 6), (3, 6)]
 
 
 def kernel(
@@ -521,10 +521,14 @@
 
         for load in loads:
             load.wait()
-        for index in range(len(rounds)):
-            pl.semaphore_wait(known.at[index], 2)
-            if index + 1 < len(rounds):
-                tell(index + 1)
+        told = [0]
+
+        def hear(count):
+            while told[0] < min(count, len(rounds)):
+                pl.semaphore_wait(known.at[told[0]], 2)
+                told[0] += 1
+                if told[0] < len(rounds):
+                    tell(told[0])
 
         def solve(which, t0, out, arrive_near, arrive_far, meanwhile, then):
             ts = (t0, a1, a2, a3)
@@ -574,6 +578,7 @@
             sums += add_up(far_terms, 3)
             for k in range(8):
                 sums_ref[pl.ds(k, 1), :] = sums[k]
+            hear(len(rounds))
             packed = pack(sums_ref[...])
             packed_ref[which] = packed
             for index, (_, shift) in enumerate(partners):
@@ -595,10 +600,12 @@
             lax.fori_loop(first, last, combine, 0, unroll=2)
 
         def arrive_near():
+            hear(1)
             wait_recv(dual_near)
             wait_recv(coef_near)
 
         def arrive_far():
+            hear(2)
             wait_recv(coef_far)
             wait_recv(dual_far)
             start(heat_halo)

time: 44.4 us -> 41.9 us (0.944)
  the two profiles are of different devices: /device:TPU:129 before, /device:TPU:1 now
where the time goes in v6:
time: 41.9 us; the launch traced here: 41.8 us
  Pallas kernels  39.8 us (95%)
  between operations  1.29 us (3%)
  local copies, waits for them, and re-layouts  0.72 us (2%)
    pallas_call x1, Pallas kernels, body(): pl.pallas_call(functools.partial(kernel, n_sec, n_slab), out_shape=jax.Sh...  39.8 us

profile of v6, /device:TPU:1, one launch (start us, length us, event | category | flops | bytes accessed | tf_op | source)
XLA Modules:
  0.0 41.8 jit_solution(17349036539541160814)
XLA Ops:
  1.3 39.8 %shard_map.86 = f32[2,4,64,128]{3,2,1,0:T(8,128)S(1)} custom-call(s32[4,48]{1,0:T(4,128)} %bitcast.7, s32[4,48]{1,0:T(4,128)} %line_hbm.1, s32[4,48]{1,0:T(4,128)} %flag_hbm.1, s32[1]{0:T(128)S(6)} %copy.9.instant_ref, f32[4,64,128]{2,1,0:T(8,128)} %bitcast.4, f32[4,64,128]{2,1,0:T(8,128)} %bitcast.5, f32[4,64,128]{2,1,0:T(8,128)} %bitcast.6), custom_call_target="tpu_custom_call" | custom-call | tf_op jit(solution)/shard_map/pallas_call | solution.py:720
  41.1 0.7 %fusion = (f32[1,4,64,128]{3,2,1,0:T(8,128)}, f32[1,4,64,128]{3,2,1,0:T(8,128)}) fusion(f32[2,4,64,128]{3,2,1,0:T(8,128)S(1)} %shard_map.86), kind=kLoop, calls=%fused_computation | loop fusion | bytes 524288 | tf_op jit(solution)/shard_map/slice | solution.py:730

commit v7 on v6

--- a/solution.py
+++ b/solution.py
@@ -11,6 +11,7 @@
 STEPS = 4
 PAIRCAP = 8
 BASIS = 4
+AHEAD = 1
 CLOSE = 4
 
 time_step = 0.1
@@ -125,6 +126,9 @@
     back,
     basis_rows,
     relay,
+    got,
+    weights,
+    weights_in,
     returned,
     sums_ref,
     packed_ref,
@@ -142,6 +146,9 @@
     known,
     relay_send,
     relay_recv,
+    ahead_send,
+    ahead_recv,
+    weight_recv,
 ):
     ingots, contact = part_hbm.shape
     melts = n_sec - ingots
@@ -153,6 +160,7 @@
     is_early = sec < early
     relayed = relays(n_sec, ingots)
     targets = sorted({m for _, m in relayed})
+    ahead = [m for m in range(AHEAD) if m < early]
     has_left, has_right = slab > 0, slab < n_slab - 1
     state_ref, adjoint_ref = both_ref.at[0], both_ref.at[1]
 
@@ -402,9 +410,28 @@
 
         passed = []
         for j in reversed(range(ingots)):
-            region = returned.at[pl.ds(first, depth), slot_rows(j)]
-            pltpu.make_async_copy(region, region, row_recv.at[j]).wait()
-            passed.append(pass_on(returned, slot_rows(j), j))
+            rows = slot_rows(j)
+
+            def arrive(j=j, rows=rows):
+                region = returned.at[pl.ds(first, depth), rows]
+                pltpu.make_async_copy(region, region, row_recv.at[j]).wait()
+
+            def add_up(j=j, rows=rows):
+                region = got.at[:, :, rows]
+                pltpu.make_async_copy(region, region, ahead_recv.at[j]).wait()
+                pltpu.make_async_copy(weights_in.at[j], weights_in.at[j], weight_recv.at[j]).wait()
+                c = [weights_in[j, i : i + 1, :] for i in range(BASIS)]
+                for z in range(depth):
+                    returned[first + z, rows, :] = (c[0] * got[0, z, rows, :] + c[1] * got[1, z, rows, :]) + (
+                        c[2] * got[2, z, rows, :] + c[3] * got[3, z, rows, :]
+                    )
+
+            if ahead:
+                pl.when(sec < len(ahead))(add_up)
+                pl.when(sec >= len(ahead))(arrive)
+            else:
+                arrive()
+            passed.append(pass_on(returned, rows, j))
 
         def add_returned(at):
             for z in range(at, at + depth):
@@ -529,6 +556,23 @@
                 told[0] += 1
                 if told[0] < len(rounds):
                     tell(told[0])
+
+        early_sends = []
+
+        def pick_basis(i):
+            t = (dual, a1, a2, a3)[i]
+            for z in range(depth):
+                basis_rows[i, z] = jnp.dot(
+                    give, t[first + z, :contact, :], precision=HIGHEST, preferred_element_type=jnp.float32
+                )
+            for m in ahead:
+                send = pltpu.make_async_remote_copy(
+                    src_ref=basis_rows.at[i, :, slot_rows(m), :],
+                    dst_ref=got.at[i, :, pl.ds(pl.multiple_of(mine * PAIRCAP, PAIRCAP), PAIRCAP), :],
+                    send_sem=ahead_send.at[m, i], recv_sem=ahead_recv.at[mine], device_id=(m, slab), device_id_type=MESH,
+                )
+                send.start()
+                early_sends.append(send)
 
         def solve(which, t0, out, arrive_near, arrive_far, meanwhile, then):
             ts = (t0, a1, a2, a3)
@@ -600,26 +644,30 @@
             lax.fori_loop(first, last, combine, 0, unroll=2)
 
         def arrive_near():
+            pick_basis(0)
             hear(1)
             wait_recv(dual_near)
             wait_recv(coef_near)
 
         def arrive_far():
+            pick_basis(1)
+            pick_basis(2)
             hear(2)
             wait_recv(coef_far)
             wait_recv(dual_far)
             start(heat_halo)
 
-        def pick_basis():
-            for i, t in enumerate((dual, a1, a2, a3)):
-                for z in range(depth):
-                    basis_rows[i, z] = jnp.dot(
-                        give, t[first + z, :contact, :], precision=HIGHEST, preferred_element_type=jnp.float32
-                    )
-
         sends = []
 
         def send_back(c):
+            weights[...] = jnp.concatenate(c + c, axis=0)
+            for m in ahead:
+                send = pltpu.make_async_remote_copy(
+                    src_ref=weights, dst_ref=weights_in.at[mine], send_sem=row_send.at[m], recv_sem=weight_recv.at[mine],
+                    device_id=(m, slab), device_id_type=MESH,
+                )
+                send.start()
+                early_sends.append(send)
             for z in range(depth):
                 back[z] = (c[0] * basis_rows[0, z] + c[1] * basis_rows[1, z]) + (
                     c[2] * basis_rows[2, z] + c[3] * basis_rows[3, z]
@@ -634,7 +682,7 @@
                         recv_sem=relay_recv.at[index], device_id=(early, slab), device_id_type=MESH,
                     ).start()
 
-            for m in range(melts):
+            for m in [m for m in range(melts) if m not in ahead]:
                 direct = [j for j in range(ingots) if (j, m) not in relayed]
                 send = pltpu.make_async_remote_copy(
                     src_ref=back.at[:, slot_rows(m), :],
@@ -647,7 +695,7 @@
                     pl.when(functools.reduce(jnp.logical_or, [mine == j for j in direct]))(lambda send=send: send.start())
                 sends.append(send)
 
-        solve(0, dual, adjoint_ref, arrive_near, arrive_far, pick_basis, send_back)
+        solve(0, dual, adjoint_ref, arrive_near, arrive_far, lambda: pick_basis(3), send_back)
 
         passed = []
         for m in range(melts):
@@ -677,7 +725,7 @@
 
         for pair in [dual_near, coef_near, dual_far, coef_far, heat_halo] + passed:
             wait_send(pair)
-        for send in sends:
+        for send in sends + early_sends:
             send.wait_send()
         for which in range(2):
             others = gather.at[which, pl.ds(0, n_slab - 1)]
@@ -705,6 +753,9 @@
         pltpu.VMEM((depth, melts * PAIRCAP, width), f32),
         pltpu.VMEM((BASIS, depth, melts * PAIRCAP, width), f32),
         pltpu.VMEM((max(len(relays(n_sec, ingots)), 1), depth, PAIRCAP, width), f32),
+        pltpu.VMEM((BASIS, depth, ingots * PAIRCAP, width), f32),
+        pltpu.VMEM((8, width), f32),
+        pltpu.VMEM((ingots, 8, width), f32),
         pltpu.VMEM((3 * depth, ingots * PAIRCAP, width), f32),
         pltpu.VMEM((8, width), f32),
         pltpu.VMEM((2, 1, width), f32),
@@ -712,7 +763,7 @@
         dma((6,)), dma((5, 2)), dma((5, 2)),
         dma((most,)), dma((most,)), dma((2, most)), dma((2,)),
         dma((2,)), dma((2,)), pltpu.SemaphoreType.REGULAR, pltpu.SemaphoreType.REGULAR((4,)),
-        dma((8,)), dma((8,)),
+        dma((8,)), dma((8,)), dma((max(AHEAD, 1), BASIS)), dma((ingots,)), dma((ingots,)),
     ]
     hbm, vmem, smem = (pl.BlockSpec(memory_space=s) for s in (pltpu.HBM, pltpu.VMEM, pltpu.SMEM))
     fields = (part[:, :, 0], line, flag, heat_level[0], material_factor[0], dual_sensitivity[0])

time: 41.9 us -> 40.6 us (0.969)
  the two profiles are of different devices: /device:TPU:1 before, /device:TPU:177 now
where the time goes in v7:
time: 40.6 us; the launch traced here: 40.5 us
  Pallas kernels  38.5 us (95%)
  between operations  1.29 us (3%)
  local copies, waits for them, and re-layouts  0.72 us (2%)
    pallas_call x1, Pallas kernels, body(): pl.pallas_call(functools.partial(kernel, n_sec, n_slab), out_shape=jax.Sh...  38.5 us

profile of v7, /device:TPU:177, one launch (start us, length us, event | category | flops | bytes accessed | tf_op | source)
XLA Modules:
  0.0 40.5 jit_solution(17285884255684982952)
XLA Ops:
  1.3 38.5 %shard_map.86 = f32[2,4,64,128]{3,2,1,0:T(8,128)S(1)} custom-call(s32[4,48]{1,0:T(4,128)} %bitcast.7, s32[4,48]{1,0:T(4,128)} %line_hbm.1, s32[4,48]{1,0:T(4,128)} %flag_hbm.1, s32[1]{0:T(128)S(6)} %copy.9.instant_ref, f32[4,64,128]{2,1,0:T(8,128)} %bitcast.4, f32[4,64,128]{2,1,0:T(8,128)} %bitcast.5, f32[4,64,128]{2,1,0:T(8,128)} %bitcast.6), custom_call_target="tpu_custom_call" | custom-call | tf_op jit(solution)/shard_map/pallas_call | solution.py:771
  39.8 0.7 %fusion = (f32[1,4,64,128]{3,2,1,0:T(8,128)}, f32[1,4,64,128]{3,2,1,0:T(8,128)}) fusion(f32[2,4,64,128]{3,2,1,0:T(8,128)S(1)} %shard_map.86), kind=kLoop, calls=%fused_computation | loop fusion | bytes 524288 | tf_op jit(solution)/shard_map/slice | solution.py:781

commit v8 on v7

--- a/solution.py
+++ b/solution.py
@@ -11,7 +11,6 @@
 STEPS = 4
 PAIRCAP = 8
 BASIS = 4
-AHEAD = 1
 CLOSE = 4
 
 time_step = 0.1
@@ -88,7 +87,13 @@
 def relays(n_sec, ingots):
     if (n_sec, ingots) != (16, 4):
         return []
-    return [(1, 5), (2, 5), (3, 5), (2, 6), (3, 6)]
+    return [(2, 6), (3, 6)]
+
+
+def ahead_of(ingots, early):
+    if early < 2:
+        return {}
+    return {0: list(range(ingots)), 1: list(range(ingots // 2, ingots))}
 
 
 def kernel(
@@ -160,7 +165,17 @@
     is_early = sec < early
     relayed = relays(n_sec, ingots)
     targets = sorted({m for _, m in relayed})
-    ahead = [m for m in range(AHEAD) if m < early]
+    ahead = ahead_of(ingots, early)
+
+    def any_of(value, choices):
+        return functools.reduce(jnp.logical_or, [value == choice for choice in choices])
+
+    def only(value, choices, count, action):
+        if len(choices) == count:
+            action()
+        elif choices:
+            pl.when(any_of(value, choices))(action)
+
     has_left, has_right = slab > 0, slab < n_slab - 1
     state_ref, adjoint_ref = both_ref.at[0], both_ref.at[1]
 
@@ -190,12 +205,18 @@
         partners.append((sum(min(step, size - step) for step, size in zip(shift, sizes)), tuple(shift)))
     partners.sort(key=lambda entry: (-entry[0], entry[1]))
 
+    digits, rest = [], slab
+    for size in reversed(sizes):
+        digits.insert(0, lax.rem(rest, size))
+        rest = lax.div(rest, size)
+    strides = [math.prod(sizes[place + 1 :]) for place in range(len(sizes))]
+    moved = [
+        [lax.rem(digit + step, size) * stride for step in range(size)]
+        for digit, size, stride in zip(digits, sizes, strides)
+    ]
+
     def partner(shift):
-        index, stride, rest = 0, 1, slab
-        for step, size in zip(reversed(shift), reversed(sizes)):
-            index = index + lax.rem(lax.rem(rest, size) + step, size) * stride
-            rest, stride = rest // size, stride * size
-        return index
+        return sum(moved[place][step] for place, step in enumerate(shift))
 
     near = sorted({offset % n_slab for offset in range(-CLOSE, CLOSE + 1)} - {0})
 
@@ -426,9 +447,10 @@
                         c[2] * got[2, z, rows, :] + c[3] * got[3, z, rows, :]
                     )
 
-            if ahead:
-                pl.when(sec < len(ahead))(add_up)
-                pl.when(sec >= len(ahead))(arrive)
+            summed = [m for m in ahead if j in ahead[m]]
+            if summed:
+                pl.when(any_of(sec, summed))(add_up)
+                pl.when(jnp.logical_not(any_of(sec, summed)))(arrive)
             else:
                 arrive()
             passed.append(pass_on(returned, rows, j))
@@ -458,7 +480,7 @@
                     wdst[z] = coef[z] * value
                 return carry
 
-            lax.fori_loop(lo, hi, plane, 0, unroll=2)
+            lax.fori_loop(lo, hi, plane, 0, unroll=hi - lo if hi - lo == 4 else 2)
             if wdst is not None:
                 clear(dst, wdst)
 
@@ -565,14 +587,14 @@
                 basis_rows[i, z] = jnp.dot(
                     give, t[first + z, :contact, :], precision=HIGHEST, preferred_element_type=jnp.float32
                 )
-            for m in ahead:
+            for place_m, m in enumerate(ahead):
                 send = pltpu.make_async_remote_copy(
                     src_ref=basis_rows.at[i, :, slot_rows(m), :],
                     dst_ref=got.at[i, :, pl.ds(pl.multiple_of(mine * PAIRCAP, PAIRCAP), PAIRCAP), :],
-                    send_sem=ahead_send.at[m, i], recv_sem=ahead_recv.at[mine], device_id=(m, slab), device_id_type=MESH,
+                    send_sem=ahead_send.at[place_m, i], recv_sem=ahead_recv.at[mine], device_id=(m, slab), device_id_type=MESH,
                 )
-                send.start()
-                early_sends.append(send)
+                only(mine, ahead[m], ingots, send.start)
+                early_sends.append((m, send))
 
         def solve(which, t0, out, arrive_near, arrive_far, meanwhile, then):
             ts = (t0, a1, a2, a3)
@@ -587,7 +609,7 @@
                     ts[k][z] = value * (2.0 / RADIUS) - ts[k - 2][z]
 
             def grow_all(k, lo, hi):
-                lax.fori_loop(lo, hi, lambda z, carry: grow(k, z) or carry, 0, unroll=2)
+                lax.fori_loop(lo, hi, lambda z, carry: grow(k, z) or carry, 0, unroll=hi - lo if hi - lo == 4 else 2)
 
             def add_up(terms, count):
                 def plane(z, sums):
@@ -666,8 +688,7 @@
                     src_ref=weights, dst_ref=weights_in.at[mine], send_sem=row_send.at[m], recv_sem=weight_recv.at[mine],
                     device_id=(m, slab), device_id_type=MESH,
                 )
-                send.start()
-                early_sends.append(send)
+                only(mine, ahead[m], ingots, send.start)
             for z in range(depth):
                 back[z] = (c[0] * basis_rows[0, z] + c[1] * basis_rows[1, z]) + (
                     c[2] * basis_rows[2, z] + c[3] * basis_rows[3, z]
@@ -682,18 +703,15 @@
                         recv_sem=relay_recv.at[index], device_id=(early, slab), device_id_type=MESH,
                     ).start()
 
-            for m in [m for m in range(melts) if m not in ahead]:
-                direct = [j for j in range(ingots) if (j, m) not in relayed]
+            for m in range(melts):
+                direct = [j for j in range(ingots) if (j, m) not in relayed and j not in ahead.get(m, [])]
                 send = pltpu.make_async_remote_copy(
                     src_ref=back.at[:, slot_rows(m), :],
                     dst_ref=returned.at[pl.ds(first, depth), pl.ds(pl.multiple_of(mine * PAIRCAP, PAIRCAP), PAIRCAP), :],
                     send_sem=row_send.at[m], recv_sem=row_recv.at[mine], device_id=(m, slab), device_id_type=MESH,
                 )
-                if len(direct) == ingots:
-                    send.start()
-                elif direct:
-                    pl.when(functools.reduce(jnp.logical_or, [mine == j for j in direct]))(lambda send=send: send.start())
-                sends.append(send)
+                only(mine, direct, ingots, send.start)
+                sends.append((m, send))
 
         solve(0, dual, adjoint_ref, arrive_near, arrive_far, lambda: pick_basis(3), send_back)
 
@@ -725,8 +743,12 @@
 
         for pair in [dual_near, coef_near, dual_far, coef_far, heat_halo] + passed:
             wait_send(pair)
-        for send in sends + early_sends:
-            send.wait_send()
+        for m, send in early_sends:
+            only(mine, ahead[m], ingots, send.wait_send)
+        for m, send in sends:
+            summed = ahead.get(m, [])
+            only(mine, summed, ingots, lambda m=m: pltpu.make_async_copy(weights, weights, row_send.at[m]).wait())
+            only(mine, [j for j in range(ingots) if j not in summed], ingots, send.wait_send)
         for which in range(2):
             others = gather.at[which, pl.ds(0, n_slab - 1)]
             pltpu.make_async_copy(others, others, sum_send.at[which]).wait()
@@ -763,7 +785,7 @@
         dma((6,)), dma((5, 2)), dma((5, 2)),
         dma((most,)), dma((most,)), dma((2, most)), dma((2,)),
         dma((2,)), dma((2,)), pltpu.SemaphoreType.REGULAR, pltpu.SemaphoreType.REGULAR((4,)),
-        dma((8,)), dma((8,)), dma((max(AHEAD, 1), BASIS)), dma((ingots,)), dma((ingots,)),
+        dma((8,)), dma((8,)), dma((4, BASIS)), dma((ingots,)), dma((ingots,)),
     ]
     hbm, vmem, smem = (pl.BlockSpec(memory_space=s) for s in (pltpu.HBM, pltpu.VMEM, pltpu.SMEM))
     fields = (part[:, :, 0], line, flag, heat_level[0], material_factor[0], dual_sensitivity[0])

time: 40.6 us -> 40 us (0.985)
  the two profiles are of different devices: /device:TPU:177 before, /device:TPU:136 now
where the time goes in v8:
time: 40 us; the launch traced here: 39.9 us
  Pallas kernels  37.9 us (95%)
  between operations  1.29 us (3%)
  local copies, waits for them, and re-layouts  0.72 us (2%)
    pallas_call x1, Pallas kernels, body(): pl.pallas_call(functools.partial(kernel, n_sec, n_slab), out_shape=jax.Sh...  37.9 us

profile of v8, /device:TPU:136, one launch (start us, length us, event | category | flops | bytes accessed | tf_op | source)
XLA Modules:
  0.0 39.9 jit_solution(9020650622895302954)
XLA Ops:
  1.3 37.9 %shard_map.86 = f32[2,4,64,128]{3,2,1,0:T(8,128)S(1)} custom-call(s32[4,48]{1,0:T(4,128)} %bitcast.7, s32[4,48]{1,0:T(4,128)} %line_hbm.1, s32[4,48]{1,0:T(4,128)} %flag_hbm.1, s32[1]{0:T(128)S(6)} %copy.9.instant_ref, f32[4,64,128]{2,1,0:T(8,128)} %bitcast.4, f32[4,64,128]{2,1,0:T(8,128)} %bitcast.5, f32[4,64,128]{2,1,0:T(8,128)} %bitcast.6), custom_call_target="tpu_custom_call" | custom-call | tf_op jit(solution)/shard_map/pallas_call | solution.py:793
  39.2 0.7 %fusion = (f32[1,4,64,128]{3,2,1,0:T(8,128)}, f32[1,4,64,128]{3,2,1,0:T(8,128)}) fusion(f32[2,4,64,128]{3,2,1,0:T(8,128)S(1)} %shard_map.86), kind=kLoop, calls=%fused_computation | loop fusion | bytes 524288 | tf_op jit(solution)/shard_map/slice | solution.py:803

commit v9 on v8

--- a/solution.py
+++ b/solution.py
@@ -90,10 +90,8 @@
     return [(2, 6), (3, 6)]
 
 
-def ahead_of(ingots, early):
-    if early < 2:
-        return {}
-    return {0: list(range(ingots)), 1: list(range(ingots // 2, ingots))}
+def ahead_of(ingots, lead):
+    return dict([(0, list(range(ingots))), (1, list(range(ingots // 2, ingots)))][:lead])
 
 
 def kernel(
@@ -157,15 +155,17 @@
 ):
     ingots, contact = part_hbm.shape
     melts = n_sec - ingots
-    early = 2 * melts // 3
+    lead = melts // 3
+    early = 2 * lead
     depth, height, width = heat_ref.shape
     first, last = depth, 2 * depth
     sec, slab = lax.axis_index("sec"), lax.axis_index("slab")
     is_melt = sec < melts
     is_early = sec < early
+    is_lead = sec < lead
     relayed = relays(n_sec, ingots)
     targets = sorted({m for _, m in relayed})
-    ahead = ahead_of(ingots, early)
+    ahead = ahead_of(ingots, lead)
 
     def any_of(value, choices):
         return functools.reduce(jnp.logical_or, [value == choice for choice in choices])
@@ -225,10 +225,14 @@
         pl.when(has_left)(lambda: greet(sec, slab - 1))
         pl.when(has_right)(lambda: greet(sec, slab + 1))
 
-        @pl.when(is_early)
+        @pl.when(is_lead)
         def _():
             for j in range(ingots):
                 greet(melts + j, slab)
+
+        @pl.when(is_early & jnp.logical_not(is_lead))
+        def _():
+            greet(sec - lead, slab)
 
         for m in targets:
             pl.when(sec == m)(lambda: greet(early, slab))
@@ -241,7 +245,7 @@
             greet(m, slab)
 
     beside = has_left.astype(jnp.int32) + has_right.astype(jnp.int32)
-    heard = jnp.where(is_melt, beside + jnp.where(is_early, 0, ingots), len(near) + early)
+    heard = jnp.where(is_melt, beside + jnp.where(is_lead, 1, jnp.where(is_early, 0, ingots)), len(near) + lead)
     heard = heard + jnp.where(sec == early, len(targets), 0) if targets else heard
     for load in tables + loads:
         load.start()
@@ -391,7 +395,17 @@
 
         for z in range(depth):
             offered[z] = jnp.dot(pick[...], state_ref[z], precision=HIGHEST, preferred_element_type=jnp.float32)
-        pl.when(is_early)(lambda: pl.semaphore_wait(ready, ingots))
+        @pl.when(is_lead)
+        def _():
+            pl.semaphore_wait(ready, ingots)
+            greet(sec + lead, slab, ready)
+            for j in range(ingots):
+                greet(melts + j, slab, ready)
+
+        @pl.when(is_early & jnp.logical_not(is_lead))
+        def _():
+            pl.semaphore_wait(ready, 1)
+
         sends = []
         for j in range(ingots):
             send = pltpu.make_async_remote_copy(
@@ -484,7 +498,9 @@
             if wdst is not None:
                 clear(dst, wdst)
 
-        @pl.when(slab % 2 == 0)
+        right_first = (slab % 2 == 0) | ((sec == 0) & (slab == 1) & has_right)
+
+        @pl.when(right_first)
         def _():
             take(returned, 1)
             add_returned(last)
@@ -499,7 +515,7 @@
             for k in (3, 2, 1, 0):
                 backward(k, first - k, first + STEPS - k)
 
-        @pl.when(slab % 2 == 1)
+        @pl.when(jnp.logical_not(right_first))
         def _():
             take(returned, 0)
             add_returned(0)
@@ -537,7 +553,7 @@
         start(coef_near)
         start(coef_far)
         start(dual_far)
-        for m in range(early):
+        for m in range(lead):
             greet(m, slab, ready)
         rounds = []
         reach = CLOSE
@@ -693,7 +709,7 @@
                 back[z] = (c[0] * basis_rows[0, z] + c[1] * basis_rows[1, z]) + (
                     c[2] * basis_rows[2, z] + c[3] * basis_rows[3, z]
                 )
-            pl.semaphore_wait(ready, melts - early)
+            pl.semaphore_wait(ready, melts - early + lead)
             for index, (j, m) in enumerate(relayed):
 
                 @pl.when(mine == j)

time: 40 us -> 39.4 us (0.985)
  the two profiles are of different devices: /device:TPU:136 before, /device:TPU:161 now
where the time goes in v9:
time: 39.4 us; the launch traced here: 39.2 us
  Pallas kernels  37.2 us (94%)
  between operations  1.29 us (3%)
  local copies, waits for them, and re-layouts  0.72 us (2%)
    pallas_call x1, Pallas kernels, body(): pl.pallas_call(functools.partial(kernel, n_sec, n_slab), out_shape=jax.Sh...  37.2 us

profile of v9, /device:TPU:161, one launch (start us, length us, event | category | flops | bytes accessed | tf_op | source)
XLA Modules:
  0.0 39.2 jit_solution(1888494715042900578)
XLA Ops:
  1.3 37.2 %shard_map.86 = f32[2,4,64,128]{3,2,1,0:T(8,128)S(1)} custom-call(s32[4,48]{1,0:T(4,128)} %bitcast.7, s32[4,48]{1,0:T(4,128)} %line_hbm.1, s32[4,48]{1,0:T(4,128)} %flag_hbm.1, s32[1]{0:T(128)S(6)} %copy.9.instant_ref, f32[4,64,128]{2,1,0:T(8,128)} %bitcast.4, f32[4,64,128]{2,1,0:T(8,128)} %bitcast.5, f32[4,64,128]{2,1,0:T(8,128)} %bitcast.6), custom_call_target="tpu_custom_call" | custom-call | tf_op jit(solution)/shard_map/pallas_call | solution.py:809
  38.5 0.7 %fusion = (f32[1,4,64,128]{3,2,1,0:T(8,128)}, f32[1,4,64,128]{3,2,1,0:T(8,128)}) fusion(f32[2,4,64,128]{3,2,1,0:T(8,128)S(1)} %shard_map.86), kind=kLoop, calls=%fused_computation | loop fusion | bytes 524288 | tf_op jit(solution)/shard_map/slice | solution.py:819

commit v10 on v9

--- a/solution.py
+++ b/solution.py
@@ -54,18 +54,21 @@
     return jnp.sum(own_lanes(values), axis=0, keepdims=True)
 
 
-def coefficients(packed):
+def unpack(packed):
     spread = own_lanes(jnp.broadcast_to(packed, (8, packed.shape[1])))
     total = jnp.broadcast_to(jnp.sum(spread, axis=1, keepdims=True), spread.shape)
-    s = [total[k : k + 1, :] for k in range(8)]
+    return [total[k : k + 1, :] for k in range(8)]
+
+
+def coefficients(packed):
+    s = unpack(packed)
     nu = [s[0], s[1], 2.0 * s[2] - s[0], 2.0 * s[3] - s[1], 2.0 * s[4] - s[0], 2.0 * s[5] - s[1], 2.0 * s[6] - s[0]]
     nu.append(4.0 * s[7] - 2.0 * s[5] - s[1])
     shift = 2.0 * CENTRE / RADIUS
     u = [shift * nu[k] + nu[k + 1] + nu[abs(k - 1)] for k in range(7)]
     mat = [[u[i + j] + u[abs(i - j)] for j in range(BASIS)] for i in range(BASIS)]
     diag = [mat[i][i] for i in range(BASIS)]
-    rhs = [(4.0 / RADIUS) * nu[i] for i in range(BASIS)]
-    inverse = []
+    inverse, factors = [], {}
     for k in range(BASIS):
         good = mat[k][k] > 1e-8 * diag[k]
         inv = jnp.where(good, 1.0 / jnp.where(good, mat[k][k], 1.0), 0.0)
@@ -74,14 +77,22 @@
             factor = mat[k][i] * inv
             for j in range(i, BASIS):
                 mat[i][j] = mat[i][j] - factor * mat[k][j]
-            rhs[i] = rhs[i] - factor * rhs[k]
-    out = [None] * BASIS
-    for i in reversed(range(BASIS)):
-        value = rhs[i]
-        for j in range(i + 1, BASIS):
-            value = value - mat[i][j] * out[j]
-        out[i] = value * inverse[i]
-    return out
+            factors[i, k] = factor
+
+    def solve(right):
+        rhs = [(4.0 / RADIUS) * value for value in right]
+        for k in range(BASIS):
+            for i in range(k + 1, BASIS):
+                rhs[i] = rhs[i] - factors[i, k] * rhs[k]
+        out = [None] * BASIS
+        for i in reversed(range(BASIS)):
+            value = rhs[i]
+            for j in range(i + 1, BASIS):
+                value = value - mat[i][j] * out[j]
+            out[i] = value * inverse[i]
+        return out
+
+    return solve(nu[:BASIS]), solve
 
 
 def relays(n_sec, ingots):
@@ -546,9 +557,9 @@
     def _():
         dual_near = halo(3, dual_ref, dual, lower(2), upper(2))
         coef_near = halo(1, factor_ref, coef, lower(1), upper(1))
-        dual_far = halo(4, dual_ref, dual, lower(depth - 2, 2), upper(depth - 3, 2))
-        coef_far = halo(2, factor_ref, coef, lower(depth - 2, 1), upper(depth - 3, 1))
-        heat_halo = halo(0, heat_ref, heat, lower(depth), upper(depth - 1))
+        dual_far = halo(4, dual_ref, dual, lower(depth - 2, 2), upper(depth - 2, 2))
+        coef_far = halo(2, factor_ref, coef, lower(depth - 2, 1), upper(depth - 2, 1))
+        heat_halo = halo(0, heat_ref, heat, lower(depth), upper(depth))
         start(dual_near)
         start(coef_near)
         start(coef_far)
@@ -649,30 +660,47 @@
             grow_all(2, first, last)
             sums = add_up(near_terms, 5)
             arrive_far()
-            for z in (first - 2, last + 1, last + 2):
+            for z in (first - 3, first - 2, last + 1, last + 2):
                 grow(1, z)
-            for z in (first - 1, last, last + 1):
+            for z in (first - 2, first - 1, last, last + 1):
                 grow(2, z)
             clear(a2)
             grow_all(3, first, last)
+            grow(3, first - 1)
             grow(3, last)
             clear(a3)
             sums += add_up(far_terms, 3)
-            for k in range(8):
-                sums_ref[pl.ds(k, 1), :] = sums[k]
             hear(len(rounds))
-            packed = pack(sums_ref[...])
-            packed_ref[which] = packed
-            for index, (_, shift) in enumerate(partners):
-                pltpu.make_async_remote_copy(
-                    src_ref=packed_ref.at[which], dst_ref=gather.at[which, pl.ds(index, 1)],
-                    send_sem=sum_send.at[which], recv_sem=sum_recv.at[which],
-                    device_id=(sec, partner(shift)), device_id_type=MESH,
-                ).start()
-            meanwhile()
-            others = gather.at[which, pl.ds(0, n_slab - 1)]
-            pltpu.make_async_copy(others, others, sum_recv.at[which]).wait()
-            c = coefficients(packed + jnp.sum(gather[which, : n_slab - 1, :], axis=0, keepdims=True))
+
+            def everywhere(slot, sums, meanwhile):
+                for k in range(8):
+                    sums_ref[pl.ds(k, 1), :] = sums[k]
+                packed = pack(sums_ref[...])
+                packed_ref[slot] = packed
+                for index, (_, shift) in enumerate(partners):
+                    pltpu.make_async_remote_copy(
+                        src_ref=packed_ref.at[slot], dst_ref=gather.at[slot, pl.ds(index, 1)],
+                        send_sem=sum_send.at[slot], recv_sem=sum_recv.at[slot],
+                        device_id=(sec, partner(shift)), device_id_type=MESH,
+                    ).start()
+                meanwhile()
+                others = gather.at[slot, pl.ds(0, n_slab - 1)]
+                pltpu.make_async_copy(others, others, sum_recv.at[slot]).wait()
+                return packed + jnp.sum(gather[slot, : n_slab - 1, :], axis=0, keepdims=True)
+
+            c, again = coefficients(everywhere(2 * which, sums, meanwhile))
+
+            def left_over(z):
+                x0, x1, x2, x3 = (ref[z] for ref in ts)
+                image = (coef[z] - (CENTRE - 6.0)) * x3 - ((a3[z - 1] + a3[z + 1]) + in_plane(x3))
+                moved = c[0] * x1 + 0.5 * (c[1] * (x2 + x0) + c[2] * (x3 + x1)) + c[3] * (image * (1.0 / RADIUS))
+                at = (c[0] * x0 + c[1] * x1) + (c[2] * x2 + c[3] * x3)
+                residual = x0 - CENTRE * at - RADIUS * moved
+                return x0 * residual, x1 * residual, x2 * residual, x3 * residual
+
+            rest = add_up(left_over, 4)
+            change = again(unpack(everywhere(2 * which + 1, rest + rest, lambda: None))[:BASIS])
+            c = [value + more for value, more in zip(c, change)]
             then(c)
 
             def combine(z, carry):
@@ -765,7 +793,7 @@
             summed = ahead.get(m, [])
             only(mine, summed, ingots, lambda m=m: pltpu.make_async_copy(weights, weights, row_send.at[m]).wait())
             only(mine, [j for j in range(ingots) if j not in summed], ingots, send.wait_send)
-        for which in range(2):
+        for which in range(4):
             others = gather.at[which, pl.ds(0, n_slab - 1)]
             pltpu.make_async_copy(others, others, sum_send.at[which]).wait()
 
@@ -796,11 +824,11 @@
         pltpu.VMEM((ingots, 8, width), f32),
         pltpu.VMEM((3 * depth, ingots * PAIRCAP, width), f32),
         pltpu.VMEM((8, width), f32),
-        pltpu.VMEM((2, 1, width), f32),
-        pltpu.VMEM((2, n_slab, width), f32),
+        pltpu.VMEM((4, 1, width), f32),
+        pltpu.VMEM((4, n_slab, width), f32),
         dma((6,)), dma((5, 2)), dma((5, 2)),
         dma((most,)), dma((most,)), dma((2, most)), dma((2,)),
-        dma((2,)), dma((2,)), pltpu.SemaphoreType.REGULAR, pltpu.SemaphoreType.REGULAR((4,)),
+        dma((4,)), dma((4,)), pltpu.SemaphoreType.REGULAR, pltpu.SemaphoreType.REGULAR((4,)),
         dma((8,)), dma((8,)), dma((4, BASIS)), dma((ingots,)), dma((ingots,)),
     ]
     hbm, vmem, smem = (pl.BlockSpec(memory_space=s) for s in (pltpu.HBM, pltpu.VMEM, pltpu.SMEM))

time: 39.4 us -> 46.4 us (1.18)
  the two profiles are of different devices: /device:TPU:161 before, /device:TPU:1 now
where the time goes in v10:
time: 46.4 us; the launch traced here: 46.3 us
  Pallas kernels  44.3 us (95%)
  between operations  1.29 us (3%)
  local copies, waits for them, and re-layouts  0.72 us (2%)
    pallas_call x1, Pallas kernels, body(): pl.pallas_call(functools.partial(kernel, n_sec, n_slab), out_shape=jax.Sh...  44.3 us

profile of v10, /device:TPU:1, one launch (start us, length us, event | category | flops | bytes accessed | tf_op | source)
XLA Modules:
  0.0 46.3 jit_solution(13185756329667042893)
XLA Ops:
  1.3 44.3 %shard_map.86 = f32[2,4,64,128]{3,2,1,0:T(8,128)S(1)} custom-call(s32[4,48]{1,0:T(4,128)} %bitcast.7, s32[4,48]{1,0:T(4,128)} %line_hbm.1, s32[4,48]{1,0:T(4,128)} %flag_hbm.1, s32[1]{0:T(128)S(6)} %copy.9.instant_ref, f32[4,64,128]{2,1,0:T(8,128)} %bitcast.4, f32[4,64,128]{2,1,0:T(8,128)} %bitcast.5, f32[4,64,128]{2,1,0:T(8,128)} %bitcast.6), custom_call_target="tpu_custom_call" | custom-call | tf_op jit(solution)/shard_map/pallas_call | solution.py:837
  45.6 0.7 %fusion = (f32[1,4,64,128]{3,2,1,0:T(8,128)}, f32[1,4,64,128]{3,2,1,0:T(8,128)}) fusion(f32[2,4,64,128]{3,2,1,0:T(8,128)S(1)} %shard_map.86), kind=kLoop, calls=%fused_computation | loop fusion | bytes 524288 | tf_op jit(solution)/shard_map/slice | solution.py:847

commit v11 on v10

--- a/solution.py
+++ b/solution.py
@@ -102,7 +102,7 @@
 
 
 def ahead_of(ingots, lead):
-    return dict([(0, list(range(ingots))), (1, list(range(ingots // 2, ingots)))][:lead])
+    return {m: list(range(ingots)) for m in range(min(3, lead))}
 
 
 def kernel(

time: 46.4 us -> 46 us (level)
  no operation moved by 1% of the time
where the time goes in v11:
time: 46 us; the launch traced here: 45.9 us
  Pallas kernels  43.9 us (95%)
  between operations  1.29 us (3%)
  local copies, waits for them, and re-layouts  0.72 us (2%)
    pallas_call x1, Pallas kernels, body(): pl.pallas_call(functools.partial(kernel, n_sec, n_slab), out_shape=jax.Sh...  43.9 us

profile of v11, /device:TPU:1, one launch (start us, length us, event | category | flops | bytes accessed | tf_op | source)
XLA Modules:
  0.0 45.9 jit_solution(8371455112641958036)
XLA Ops:
  1.3 43.9 %shard_map.86 = f32[2,4,64,128]{3,2,1,0:T(8,128)S(1)} custom-call(s32[4,48]{1,0:T(4,128)} %bitcast.7, s32[4,48]{1,0:T(4,128)} %line_hbm.1, s32[4,48]{1,0:T(4,128)} %flag_hbm.1, s32[1]{0:T(128)S(6)} %copy.9.instant_ref, f32[4,64,128]{2,1,0:T(8,128)} %bitcast.4, f32[4,64,128]{2,1,0:T(8,128)} %bitcast.5, f32[4,64,128]{2,1,0:T(8,128)} %bitcast.6), custom_call_target="tpu_custom_call" | custom-call | tf_op jit(solution)/shard_map/pallas_call | solution.py:837
  45.1 0.7 %fusion = (f32[1,4,64,128]{3,2,1,0:T(8,128)}, f32[1,4,64,128]{3,2,1,0:T(8,128)}) fusion(f32[2,4,64,128]{3,2,1,0:T(8,128)S(1)} %shard_map.86), kind=kLoop, calls=%fused_computation | loop fusion | bytes 524288 | tf_op jit(solution)/shard_map/slice | solution.py:847
